TPU v7x, 128 devices: a whole 4x4x4 slice. The times are simulated.
128 devices in a mesh: section: 2 (over x_hi), ctx: 16 (over x_lo, z, core), fsdp: 4 (over y).
Axes of the slice: x: 4 (x_hi: 2, x_lo: 2; x = x_hi * 2 + x_lo), y: 4, z: 4, core: 2. Of those that a mesh axis runs over, the one named last changes fastest.
Arguments:
- inputs: bfloat16 [2, 4, 2048, 768], P(None, 'fsdp', 'ctx'), may hold values from -6 to 6
- out_grad: bfloat16 [2, 4, 2048, 768], P(None, 'fsdp', 'ctx'), may hold values from -6 to 6
- doc_lengths: int32 [2, 4, 4], P(None, 'fsdp'), may hold values from 0 to 2048, as said below
- attn_gain: bfloat16 [2, 768], P('section', 'fsdp'), may hold values from 0.099609375 to 1.8984375
- qkv_weight: bfloat16 [2, 768, 2304], P('section', 'fsdp'), may hold values from -0.21875 to 0.21875
- proj_weight: bfloat16 [2, 768, 768], P('section', 'fsdp'), may hold values from -1.25 to 1.25
- mlp_gain: bfloat16 [2, 768], P('section', 'fsdp'), may hold values from 0.099609375 to 1.8984375
- lift_weight: bfloat16 [2, 768, 2304], P('section', 'fsdp'), may hold values from -0.21875 to 0.21875
- down_weight: bfloat16 [2, 1152, 768], P('section', 'fsdp'), may hold values from -0.1875 to 0.1875
Outputs:
- acts: bfloat16 [2, 2, 4, 2048, 768], P('section', None, 'fsdp', 'ctx')
- in_grads: bfloat16 [2, 2, 4, 2048, 768], P('section', None, 'fsdp', 'ctx')
- attn_gain_grad: float32 [2, 768], P('section', 'fsdp')
- qkv_grad: float32 [2, 768, 2304], P('section', 'fsdp')
- proj_grad: float32 [2, 768, 768], P('section', 'fsdp')
- mlp_gain_grad: float32 [2, 768], P('section', 'fsdp')
- lift_grad: float32 [2, 768, 2304], P('section', 'fsdp')
- down_grad: float32 [2, 1152, 768], P('section', 'fsdp')
Inputs may be any that keep to these rules, and one draw needn't show every extreme that they name: `doc_lengths`: each sequence's 4 document lengths sum to 2048; some may be zero; one sequence, chosen at random, is a single document.
All inputs are finite; a program needn't handle non-finite values.
Results may differ from a plain program's by a relative error of at most 0.035.
Values may be sent and summed in bfloat16 or wider, within the bound.
No kernel may reach another device: no remote copies, remote signals or barrier semaphores. Data moves between devices by JAX's collectives and lax.ppermute only.
A program may use at most 128 MiB of HBM per device.

v0:
```python
import functools

import jax
import jax.numpy as jnp
from jax import lax
from jax.experimental import pallas as pl
from jax.experimental.pallas import tpu as pltpu
from jax.sharding import PartitionSpec as P

D = 768
HD = 64
HALF = 64
SEQ_LEN = 2048
FF = 1152
WIDE = 2304
ROWS = 128
EXT = ROWS + 2 * HALF
MICRO = 2
OWN = MICRO * ROWS
SHARDS = 4
TILES = D // 128
GROUP = 2
norm_eps = 1e-05
rope_base = 10000.0
masked_score = -1e30
root_half = 0.7071067811865476
inv_root_tau = 0.3989422804014327
F32 = jnp.float32
BF16 = jnp.bfloat16


def mm(left, right):
    return lax.dot_general(left, right, (((1,), (0,)), ((), ())), preferred_element_type=F32)


def mm_nt(left, right):
    return lax.dot_general(left, right, (((1,), (1,)), ((), ())), preferred_element_type=F32)


def mm_tn(left, right):
    return lax.dot_general(left, right, (((0,), (0,)), ((), ())), preferred_element_type=F32)


def norm_parts(hidden):
    centre = hidden - jnp.mean(hidden, axis=-1, keepdims=True)
    inv_scale = lax.rsqrt(jnp.mean(centre * centre, axis=-1, keepdims=True) + norm_eps)
    return centre * inv_scale, inv_scale


def norm_back(grad_out, gain, normed, inv_scale):
    grad_normed = grad_out * gain
    inner = (
        grad_normed
        - jnp.mean(grad_normed, axis=-1, keepdims=True)
        - normed * jnp.mean(grad_normed * normed, axis=-1, keepdims=True)
    )
    return inner * inv_scale


def lane_is_low(shape, period):
    return lax.broadcasted_iota(jnp.int32, shape, 1) % period < period // 2


def turn(x):
    return jnp.where(lane_is_low(x.shape, HD), pltpu.roll(x, 96, 1), pltpu.roll(x, 32, 1))


def rotate(x, cosine, sine):
    return x * cosine + turn(x) * sine


def rotate_back(x, cosine, sine):
    return x * cosine - turn(x) * sine


def stack_heads(x):
    low = lane_is_low(x.shape, 128)
    zero = jnp.zeros_like(x)
    return jnp.concatenate([jnp.where(low, x, zero), jnp.where(low, zero, x)], axis=0)


def join_heads(x):
    half = x.shape[0] // 2
    low = lane_is_low((half, 128), 128)
    return jnp.where(low, x[:half], x[half:])


def start_weights(sources, buffers, sems):
    waits = {}
    for index, (name, source) in enumerate(sources.items()):
        copy = pltpu.make_async_copy(source, buffers[name], sems.at[index])
        copy.start()
        waits[name] = [copy]
    return waits


def finish(waits, name):
    for copy in waits[name]:
        copy.wait()


def load_stream(flag, own, low, high, other, ext):
    for m in range(MICRO):
        for ref, alt, start, size in (
            (low, other[1], 0, HALF),
            (own, other[0], HALF, ROWS),
            (high, other[2], HALF + ROWS, HALF),
        ):
            value = ref[m]
            if alt is not None:
                value = jnp.where(flag, value, alt[m])
            ext[pl.ds(m * EXT + start, size), :] = value


def own_rows(x):
    return jnp.concatenate([x[HALF : HALF + ROWS], x[EXT + HALF : EXT + HALF + ROWS]], axis=0)


def repeat(count, step):
    lax.fori_loop(0, count, lambda i, carry: (step(i), carry)[1], 0)


def span(start, size, unit=128):
    return pl.ds(pl.multiple_of(start, unit), size)


def by_tiles(unit):
    def step(i):
        for j in range(GROUP):
            unit(i * GROUP + j)

    repeat(TILES // GROUP, step)


def norm_rows(source, gain, target):
    def step(i):
        rows = span(i * 128, 128)
        normed, _ = norm_parts(source[rows, :].astype(F32))
        target[rows, :] = (normed * gain).astype(BF16)

    repeat(source.shape[0] // 128, step)


def forward_attention(ext, gain, wqkv, cos_ref, sin_ref, bias_ref, a_ext, q_ref, k_ref, v_ref, p_ref, o_ref):
    norm_rows(ext, gain, a_ext)
    a_own = o_ref
    a_own[...] = own_rows(a_ext[...])
    own_span = pl.ds(HALF, ROWS)

    def project(t):
        cols = span(256 * t, 256)
        queries = mm(a_own[...], wqkv[:, cols])
        keys = mm(a_ext[...], wqkv[:, span(D + 256 * t, 256)])
        v_ref[:, cols] = mm(a_ext[...], wqkv[:, span(2 * D + 256 * t, 256)]).astype(BF16)
        for s in range(2):
            tile, lanes = span(256 * t + 128 * s, 128), slice(128 * s, 128 * s + 128)
            for m in range(MICRO):
                part = queries[m * ROWS : (m + 1) * ROWS, lanes]
                turned = rotate(part, cos_ref[own_span, :], sin_ref[own_span, :]).astype(BF16)
                q_ref[pl.ds(m * ROWS, ROWS), tile] = turned * jnp.asarray(0.125, BF16)
                part = keys[m * EXT : (m + 1) * EXT, lanes]
                k_ref[pl.ds(m * EXT, EXT), tile] = rotate(part, cos_ref[...], sin_ref[...]).astype(BF16)

    repeat(3, project)

    def unit(t):
        cols = pl.ds(pl.multiple_of(t * 128, 128), 128)
        for m in range(MICRO):
            q2 = stack_heads(q_ref[pl.ds(m * ROWS, ROWS), cols])
            scores = mm_nt(k_ref[pl.ds(m * EXT, EXT), cols], q2) + bias_ref[m]
            terms = jnp.exp(scores - jnp.max(scores, axis=0, keepdims=True))
            probs = (terms * (1.0 / jnp.sum(terms, axis=0, keepdims=True))).astype(BF16)
            p_ref[m, t] = probs
            attended = mm_tn(probs, v_ref[pl.ds(m * EXT, EXT), cols])
            o_ref[pl.ds(m * ROWS, ROWS), cols] = join_heads(attended).astype(BF16)

    by_tiles(unit)


def forward_mlp(own, o_ref, wproj, mlp_gain, wlift, wdown, h2_ref, b_ref, m_ref, left_ref, right_ref, h3_ref, waits):
    finish(waits, "proj")

    def mix(t):
        cols = span(256 * t, 256)
        added = mm(o_ref[...], wproj[:, cols])
        for m in range(MICRO):
            rows = pl.ds(m * ROWS, ROWS)
            h2_ref[rows, cols] = own[m, :, cols].astype(F32) + added[m * ROWS : (m + 1) * ROWS]

    repeat(3, mix)
    norm_rows(h2_ref, mlp_gain, b_ref)
    finish(waits, "lift")

    def lift(t):
        cols = span(384 * t, 384)
        gate = mm(b_ref[...], wlift[:, cols])
        up = mm(b_ref[...], wlift[:, span(FF + 384 * t, 384)])
        cdf = 0.5 * (1.0 + lax.erf(gate * root_half))
        gelu = gate * cdf
        m_ref[:, cols] = (gelu * up).astype(BF16)
        if left_ref is not None:
            pdf = jnp.exp(-0.5 * gate * gate) * inv_root_tau
            left_ref[:, cols] = up * (cdf + gate * pdf)
            right_ref[:, cols] = gelu

    repeat(3, lift)
    finish(waits, "down")

    def down(t):
        cols = span(256 * t, 256)
        h3 = (h2_ref[:, cols] + mm(m_ref[...], wdown[:, cols])).astype(BF16)
        for m in range(MICRO):
            h3_ref[m, :, cols] = h3[m * ROWS : (m + 1) * ROWS]

    repeat(3, down)


def backward_mlp(grad_ref, h2_ref, mlp_gain, wproj, wlift, wdown, left_ref, right_ref, du_ref, gb_ref, do_ref,
                 dh2_ref, b_ref, mlp_ref):
    def lift(t):
        cols = span(384 * t, 384)
        dm = mm_nt(grad_ref[...], wdown[cols, :])
        du_ref[:, cols] = (dm * left_ref[:, cols]).astype(BF16)
        du_ref[:, span(FF + 384 * t, 384)] = (dm * right_ref[:, cols]).astype(BF16)

    repeat(3, lift)

    def source(t):
        rows = span(256 * t, 256)
        dh2_ref[:, rows] = mm_nt(du_ref[...], wlift[rows, :])

    repeat(3, source)
    if mlp_ref is not None:
        mlp_ref[...] = jnp.zeros_like(mlp_ref)

    def norm(i):
        rows = span(i * 128, 128)
        db = dh2_ref[rows, :]
        normed, inv_scale = norm_parts(h2_ref[rows, :])
        dh2 = grad_ref[rows, :].astype(F32) + norm_back(db, mlp_gain, normed, inv_scale)
        dh2_ref[rows, :] = dh2
        gb_ref[rows, :] = dh2.astype(BF16)
        if mlp_ref is not None:
            mlp_ref[...] += jnp.sum(db * normed, axis=0, keepdims=True)
            b_ref[rows, :] = (normed * mlp_gain).astype(BF16)

    repeat(2, norm)

    def attended(t):
        rows = span(256 * t, 256)
        do_ref[:, rows] = mm_nt(gb_ref[...], wproj[rows, :]).astype(BF16)

    repeat(3, attended)


def backward_attention(q_ref, k_ref, v_ref, p_ref, do_ref, cos_ref, sin_ref, dq_ref, dkv_ref, low_ref, high_ref):
    cosine, sine = cos_ref[...], sin_ref[...]
    cos_own, sin_own = cosine[HALF : HALF + ROWS], sine[HALF : HALF + ROWS]

    def unit(t):
        cols = pl.ds(pl.multiple_of(t * 128, 128), 128)
        value_cols = pl.ds(pl.multiple_of(D + t * 128, 128), 128)
        for m in range(MICRO):
            rows = pl.ds(m * ROWS, ROWS)
            q2 = stack_heads(q_ref[rows, cols])
            do2 = stack_heads(do_ref[rows, cols])
            probs = p_ref[m, t]
            dprobs = mm_nt(v_ref[pl.ds(m * EXT, EXT), cols], do2)
            wide = probs.astype(F32)
            inner = jnp.sum(wide * dprobs, axis=0, keepdims=True)
            ds = (wide * (dprobs - inner)).astype(BF16)
            dq = join_heads(mm_tn(ds, k_ref[pl.ds(m * EXT, EXT), cols])) * 0.125
            dq_ref[rows, cols] = rotate_back(dq, cos_own, sin_own).astype(BF16)
            dk = rotate_back(mm(ds, q2), cosine, sine)
            dv = mm(probs, do2)
            for grad, where in ((dk, cols), (dv, value_cols)):
                low_ref[m, :, where] = grad[:HALF].astype(BF16)
                dkv_ref[rows, where] = grad[HALF : HALF + ROWS]
                high_ref[m, :, where] = grad[HALF + ROWS :].astype(BF16)

    by_tiles(unit)


def place_shards(index, own, first, first_other, second, second_other, put):
    f, core = index[1], index[2]
    put(own, f, None)
    put(first, lax.rem(f + 3 + 2 * core, 4), None)
    put(first_other, lax.rem(f + 1 + 2 * core, 4), None)
    put(second, lax.rem(f + 2, 4), core)
    put(second_other, lax.rem(f + 2, 4), 1 - core)


def pack_qkv_kernel(index, qkv, gains, own, whole, half, first_rows, last_rows, sems):
    rows = pl.ds(pl.multiple_of(index[2] * 96, 16), 96)
    copies = [
        pltpu.make_async_copy(src, dst, sems.at[n])
        for n, (src, dst) in enumerate((
            (qkv, whole.at[:, pl.ds(0, WIDE)]),
            (gains, whole.at[pl.ds(0, 16), pl.ds(WIDE, 128)]),
            (qkv.at[rows], half.at[:, pl.ds(0, WIDE)]),
            (gains, half.at[pl.ds(0, 16), pl.ds(WIDE, 128)]),
            (own.at[:, pl.ds(0, HALF)], first_rows),
            (own.at[:, pl.ds(ROWS - HALF, HALF)], last_rows),
        ))
    ]
    for copy in copies:
        copy.start()
    for copy in copies:
        copy.wait()


def pack_kernel(index, lift, proj, down, rest, rest_half, sems):
    core = index[2]
    copies = []

    def go(src, dst):
        copy = pltpu.make_async_copy(src, dst, sems.at[len(copies)])
        copy.start()
        copies.append(copy)

    half = lambda size: pl.ds(pl.multiple_of(core * size, 16), size)
    go(lift, rest.at[pl.ds(0, 192)])
    go(lift.at[half(96)], rest_half.at[pl.ds(0, 96)])
    for block in range(3):
        cols = pl.ds(block * D, D)
        go(proj.at[pl.ds(64 * block, 64)], rest.at[pl.ds(192, 64), cols])
        go(down.at[pl.ds(96 * block, 96)], rest.at[pl.ds(256, 96), cols])
        go(
            proj.at[pl.ds(pl.multiple_of(64 * block + core * 32, 16), 32)],
            rest_half.at[pl.ds(96, 32), cols],
        )
        go(
            down.at[pl.ds(pl.multiple_of(96 * block + core * 48, 16), 48)],
            rest_half.at[pl.ds(128, 48), cols],
        )
    for copy in copies:
        copy.wait()


def gather_gain(tiles, row):
    parts = []
    for tile in tiles:
        parts += [tile[row : row + 1, :], tile[row + 1 : row + 2, :64]]
    return jnp.concatenate(parts, axis=1)


def forward_attention_kernel(index, own, low, high, gain_tile, cos_ref, sin_ref, bias_ref,
                             shard, first, first_other, second, second_other,
                             o, gains, whole, wqkv, tiles, ext, a_ext, q, k, v, p, sems, out_sem):
    copies = []

    def go(src, dst):
        copy = pltpu.make_async_copy(src, dst, sems.at[len(copies)])
        copy.start()
        copies.append(copy)

    def put(piece, f, half):
        at, size = (f * 192, 192) if half is None else (f * 192 + half * 96, 96)
        rows = pl.ds(pl.multiple_of(at, 16), size)
        go(piece if piece is shard else piece.at[:, pl.ds(0, WIDE)], wqkv.at[rows])
        if piece is not shard and piece is not second_other:
            go(piece.at[pl.ds(0, 16), pl.ds(WIDE, 128)], tiles.at[f])

    place_shards(index, shard, first, first_other, second, second_other, put)
    go(gain_tile, tiles.at[index[1]])
    load_stream(None, own, low, high, (None, None, None), ext)
    for copy in copies:
        copy.wait()
    out = pltpu.make_async_copy(wqkv, whole, out_sem)
    out.start()
    shards = [tiles[f].astype(F32) for f in range(SHARDS)]
    gains[0:1, :] = gather_gain(shards, 0)
    gains[1:2, :] = gather_gain(shards, 2)
    forward_attention(ext, gains[0:1], wqkv, cos_ref, sin_ref, bias_ref, a_ext, q, k, v, p, o)
    out.wait()


def forward_mlp_kernel(index, own, o, gains, lift, proj, down, first, first_other, second, second_other,
                       h3_ref, whole_proj, whole_lift, whole_down, wproj, wlift, wdown, h2, b, m_out, sems):
    waits = {"proj": [], "lift": [], "down": []}
    count = [0]

    def go(name, src, dst):
        copy = pltpu.make_async_copy(src, dst, sems.at[count[0]])
        copy.start()
        count[0] += 1
        waits[name].append(copy)

    f = index[1]

    def put(piece, s, half):
        rows = lambda at, size: pl.ds(pl.multiple_of(at, 16), size)
        if piece is None:
            go("proj", proj, wproj.at[rows(f * 192, 192)])
            go("lift", lift, wlift.at[rows(f * 192, 192)])
            go("down", down, wdown.at[rows(f * 288, 288)])
            return
        n = 2 if half is None else 1
        h = 0 if half is None else half
        go("lift", piece.at[pl.ds(0, 96 * n)], wlift.at[rows(s * 192 + h * 96, 96 * n)])
        for b in range(3):
            cols = pl.ds(b * D, D)
            go("proj", piece.at[pl.ds(96 * n, 32 * n), cols], wproj.at[rows(s * 192 + b * 64 + h * 32, 32 * n)])
            go("down", piece.at[pl.ds(128 * n, 48 * n), cols], wdown.at[rows(s * 288 + b * 96 + h * 48, 48 * n)])

    place_shards(index, None, first, first_other, second, second_other, put)
    outs = []
    for name, buffer, whole in (("proj", wproj, whole_proj), ("lift", wlift, whole_lift), ("down", wdown, whole_down)):
        finish(waits, name)
        copy = pltpu.make_async_copy(buffer, whole, sems.at[count[0]])
        copy.start()
        count[0] += 1
        outs.append(copy)
        waits[name] = []
    forward_mlp(own, o, wproj, gains[1:2], wlift, wdown, h2, b, m_out, None, None, h3_ref, waits)
    for copy in outs:
        copy.wait()


def start_all(pairs, sems, first):
    copies = [pltpu.make_async_copy(src, dst, sems.at[first + n]) for n, (src, dst) in enumerate(pairs)]
    for copy in copies:
        copy.start()
    return copies


def turning_kernel(flag_ref, own, low, high, other_own, other_low, other_high, cotangent, gains,
                   cos_ref, sin_ref, bias_ref, qkv_hbm, proj_hbm, lift_hbm, down_hbm, *refs):
    kept, (dh2_ref, dq, dkv, to_low, to_high) = refs[:11], refs[11:16]
    wqkv, wproj, wlift, wdown, ext, a_ext, mine, du, do, h3_ref, q, k, v, p, o, h2, m_out, left, right, src, sems = refs[16:]
    waits = start_weights(
        {"qkv": qkv_hbm, "proj": proj_hbm, "lift": lift_hbm, "down": down_hbm},
        {"qkv": wqkv, "proj": wproj, "lift": wlift, "down": wdown}, sems,
    )
    flag = flag_ref[0] == 1
    load_stream(flag, own, low, high, (other_own, other_low, other_high), ext)
    for m in range(MICRO):
        mine[m] = ext[pl.ds(m * EXT + HALF, ROWS), :]
        src[pl.ds(m * ROWS, ROWS), :] = mine[m]
    finish(waits, "qkv")
    forward_attention(ext, gains[0:1], wqkv, cos_ref, sin_ref, bias_ref, a_ext, q, k, v, p, o)
    outs = start_all(zip((q, k, v, p, o, src), kept[1:6] + kept[10:]), sems, 4)
    spare = a_ext.at[pl.ds(0, OWN)]
    forward_mlp(mine, o, wproj, gains[1:2], wlift, wdown, h2, spare, m_out, left, right, h3_ref, waits)
    outs += start_all(zip((h3_ref, h2, m_out, left, right), kept[:1] + kept[6:10]), sems, 10)
    grad = a_ext.at[pl.ds(OWN, OWN)]
    for m in range(MICRO):
        grad[pl.ds(m * ROWS, ROWS), :] = cotangent[m]
    backward_mlp(grad, h2, gains[1:2], wproj, wlift, wdown, left, right, du, spare, do, dh2_ref, None, None)
    backward_attention(q, k, v, p, do, cos_ref, sin_ref, dq, dkv, to_low, to_high)
    for copy in outs:
        copy.wait()


def back_kernel(flag_ref, incoming, cotangent, gains, cos_ref, sin_ref, proj_hbm, lift_hbm, down_hbm,
                q_hbm, k_hbm, v_hbm, p_hbm, h2_hbm, left_hbm, right_hbm, *refs):
    kept, (mlp_ref, dh2_ref, dq, dkv, to_low, to_high) = refs[:4], refs[4:10]
    wproj, wlift, wdown, do, q, k, v, p, h2, left, right, grad_ref, du, gb_ref, b_ref, sems = refs[10:]
    early = start_all(
        ((down_hbm, wdown), (left_hbm, left), (right_hbm, right), (lift_hbm, wlift), (h2_hbm, h2), (proj_hbm, wproj)),
        sems, 0,
    )
    late = start_all(((q_hbm, q), (v_hbm, v), (p_hbm, p), (k_hbm, k)), sems, 6)
    flag = flag_ref[0] == 1
    for m in range(MICRO):
        grad_ref[pl.ds(m * ROWS, ROWS), :] = jnp.where(flag, incoming[m], cotangent[m])
    for copy in early:
        copy.wait()
    backward_mlp(
        grad_ref, h2, gains[1:2], wproj, wlift, wdown, left, right, du, gb_ref, do, dh2_ref, b_ref, mlp_ref
    )
    outs = start_all(zip((grad_ref, du, gb_ref, b_ref), kept), sems, 10)
    for copy in late:
        copy.wait()
    backward_attention(q, k, v, p, do, cos_ref, sin_ref, dq, dkv, to_low, to_high)
    for copy in outs:
        copy.wait()


def joined_grads(dq, dkv, from_low, from_high, dqkv):
    dqkv[:, :D] = dq[...]
    for m in range(MICRO):
        first, last = pl.ds(m * ROWS, HALF), pl.ds(m * ROWS + HALF, HALF)
        dqkv[first, D:] = (dkv[first, :] + from_low[m].astype(F32)).astype(BF16)
        dqkv[last, D:] = (dkv[last, :] + from_high[m].astype(F32)).astype(BF16)


def source_kernel(src, gains, dh2, dq, dkv, from_low, from_high, qkv_hbm, out_ref, wqkv, dqkv, sems):
    waits = start_weights({"qkv": qkv_hbm}, {"qkv": wqkv}, sems)
    joined_grads(dq, dkv, from_low, from_high, dqkv)
    normed, inv_scale = norm_parts(src[...].astype(F32))
    finish(waits, "qkv")
    da = mm_nt(dqkv[...], wqkv[...])
    dh = dh2[...] + norm_back(da, gains[0:1], normed, inv_scale)
    for m in range(MICRO):
        out_ref[m] = dh[m * ROWS : (m + 1) * ROWS].astype(BF16)


def gain_block(attn, mlp, f):
    rows = []
    for gain in (attn, mlp):
        rows.append(gain[:, 192 * f : 192 * f + 128])
        rows.append(jnp.concatenate([gain[:, 192 * f + 128 : 192 * f + 192], jnp.zeros((1, 64), F32)], axis=1))
    return jnp.concatenate(rows + [jnp.zeros((92, 128), F32)], axis=0).astype(BF16)


def source_grad_kernel(index, src, gains, dh2, dq, dkv, from_low, from_high, mlp_grad, qkv_hbm,
                       out_ref, keep, send, wqkv, dqkv, qkv_ref, gain_ref, sems):
    waits = start_weights({"qkv": qkv_hbm}, {"qkv": wqkv}, sems)
    joined_grads(dq, dkv, from_low, from_high, dqkv)
    normed, inv_scale = norm_parts(src[...].astype(F32))
    finish(waits, "qkv")
    da = mm_nt(dqkv[...], wqkv[...])
    attn_grad = jnp.sum(da * normed, axis=0, keepdims=True)
    mlp = mlp_grad[...]
    for f in range(SHARDS):
        gain_ref[f] = gain_block(attn_grad, mlp, f)
    a = (normed * gains[0:1]).astype(BF16)
    for t in range(9):
        cols = pl.ds(256 * t, 256)
        qkv_ref[:, cols] = mm_tn(a, dqkv[:, cols]).astype(BF16)
    copies = []
    for target, half in ((send, 1 - index[2]), (keep, index[2])):
        for f in range(SHARDS):
            rows = pl.ds(pl.multiple_of(f * 192 + half * 96, 16), 96)
            for src_ref, dst_ref in (
                (qkv_ref.at[rows], target.at[f, :, pl.ds(0, WIDE)]),
                (gain_ref.at[f], target.at[f, :, pl.ds(WIDE, 128)]),
            ):
                copy = pltpu.make_async_copy(src_ref, dst_ref, sems.at[1 + len(copies)])
                copy.start()
                copies.append(copy)
    dh = dh2[...] + norm_back(da, gains[0:1], normed, inv_scale)
    for m in range(MICRO):
        out_ref[m] = dh[m * ROWS : (m + 1) * ROWS].astype(BF16)
    for copy in copies:
        copy.wait()


def weight_grad_kernel(index, m_ref, grad_ref, b_ref, du, o_ref, gb_ref, keep, send,
                       down_ref, lift_ref, proj_ref, pad_ref, sems):
    core = index[2]
    copies = []

    def go(src, dst):
        copy = pltpu.make_async_copy(src, dst, sems.at[len(copies)])
        copy.start()
        copies.append(copy)

    sides = ((send, 1 - core), (keep, core))
    rows = lambda at, size: pl.ds(pl.multiple_of(at, 16), size)
    pad_ref[...] = jnp.zeros_like(pad_ref)
    for target, _ in sides:
        for f in range(SHARDS):
            go(pad_ref, target.at[f, pl.ds(176, 16)])
    for t in range(9):
        cols = pl.ds(256 * t, 256)
        lift_ref[:, cols] = mm_tn(b_ref[...], du[:, cols]).astype(BF16)
    for target, half in sides:
        for f in range(SHARDS):
            go(lift_ref.at[rows(f * 192 + half * 96, 96)], target.at[f, pl.ds(0, 96)])
    for t in range(3):
        cols = pl.ds(256 * t, 256)
        down_ref[:, cols] = mm_tn(m_ref[...], grad_ref[:, cols]).astype(BF16)
        proj_ref[:, cols] = mm_tn(o_ref[...], gb_ref[:, cols]).astype(BF16)
    for target, half in sides:
        for f in range(SHARDS):
            for b in range(3):
                cols = pl.ds(b * D, D)
                go(proj_ref.at[rows(f * 192 + b * 64 + half * 32, 32)], target.at[f, pl.ds(96, 32), cols])
                go(down_ref.at[rows(f * 288 + b * 96 + half * 48, 48)], target.at[f, pl.ds(128, 48), cols])
    for copy in copies:
        copy.wait()


def add_up(parts):
    total = parts[0].astype(F32)
    for part in parts[1:]:
        total = total + part.astype(F32)
    return total.astype(BF16)


def rest_core_kernel(index, keep, other, *outs):
    for d, out in enumerate(outs):
        rows = pl.ds(pl.multiple_of(lax.rem(index[0] + d, 4) * 48, 16), 48)
        for f in range(SHARDS):
            out[f] = add_up([keep[f, rows, :], other[f, rows, :]])


def rest_z_kernel(index, own, a, b, c, *outs):
    for d, out in enumerate(outs):
        f = lax.rem(index[1] + d, 4)
        out[...] = add_up([own[f], a[f], b[f], c[f]])


def qkv_core_kernel(index, keep, other, *outs):
    for d, out in enumerate(outs):
        f = lax.rem(index[1] + d, 4)
        out[...] = add_up([keep[f], other[f]])


def qkv_y_kernel(index, own, a, b, c, out_0, out_1, out_2, out_3, total):
    total[...] = add_up([own[...], a[...], b[...], c[...]])
    for d, out in enumerate((out_0, out_1, out_2, out_3)):
        z = lax.rem(index[0] + d, 4)
        rows = pl.ds(pl.multiple_of(lax.div(z, 2) * 48, 16), 48)
        cols = pl.ds(pl.multiple_of(lax.rem(z, 2) * 1152, 128), 1152)
        out[:, pl.ds(0, 1152)] = total[rows, cols]
        out[:, pl.ds(1152, 128)] = total[pl.ds(0, 48), pl.ds(WIDE, 128)]


def joint_kernel(r0, r1, r2, r3, q0, q1, q2, q3, out):
    out[:, pl.ds(0, WIDE)] = add_up([r0[...], r1[...], r2[...], r3[...]])
    out[:, pl.ds(WIDE, 1280)] = add_up([q0[...], q1[...], q2[...], q3[...]])


def pair_kernel(a, b, out):
    out[...] = add_up([a[...], b[...]])


def final_kernel(index, *refs):
    pieces, (qkv_out, proj_out, lift_out, down_out, gain_out, rest) = refs[:8], refs[8:]
    core = index[2]
    for side in range(2):
        half = core if side == 0 else 1 - core
        for d in range(4):
            piece = pieces[4 * side + d]
            z = lax.rem(index[0] - d + 4, 4)
            rest[side, pl.ds(pl.multiple_of(z * 48, 16), 48), :] = piece[:, pl.ds(0, WIDE)]
            qkv_out[
                pl.ds(pl.multiple_of(half * 96 + lax.div(z, 2) * 48, 16), 48),
                pl.ds(pl.multiple_of(lax.rem(z, 2) * 1152, 128), 1152),
            ] = piece[:, pl.ds(WIDE, 1152)].astype(F32)
        rows = lambda at, size: pl.ds(pl.multiple_of(at, 16), size)
        lift_out[rows(half * 96, 96), :] = rest[side, pl.ds(0, 96), :].astype(F32)
        for b in range(3):
            cols = pl.ds(b * D, D)
            proj_out[rows(b * 64 + half * 32, 32), :] = rest[side, pl.ds(96, 32), cols].astype(F32)
            down_out[rows(b * 96 + half * 48, 48), :] = rest[side, pl.ds(128, 48), cols].astype(F32)
    gain_out[...] = pieces[0][pl.ds(0, 16), pl.ds(WIDE + 1152, 128)].astype(F32)


def call(kernel, name, ins, outs, scratch, flops, limit=24):
    places = {"v": pltpu.VMEM, "a": pl.ANY, "s": pltpu.SMEM}
    return pl.pallas_call(
        kernel,
        name=name,
        out_shape=[jax.ShapeDtypeStruct(out[0], out[1]) for out in outs],
        in_specs=[pl.BlockSpec(memory_space=places[place]) for _, place in ins],
        out_specs=[pl.BlockSpec(memory_space=places[out[2] if len(out) > 2 else "v"]) for out in outs],
        scratch_shapes=scratch,
        compiler_params=pltpu.CompilerParams(vmem_limit_bytes=limit * 2**20),
        cost_estimate=pl.CostEstimate(flops=flops, bytes_accessed=flops // 300, transcendentals=0),
    )(*[array for array, _ in ins])


def travel(block, target):
    pairs = []
    for ctx in range(16):
        for f in range(SHARDS):
            xlo, z, core, g = target(ctx // 8, ctx // 2 % 4, ctx % 2, f)
            pairs.append((ctx * SHARDS + f, (xlo * 8 + z % 4 * 2 + core) * SHARDS + g % 4))
    return lax.ppermute(block, ("ctx", "fsdp"), pairs)


def along_y(block, d):
    return travel(block, lambda x, z, c, f: (x, z, c, f + d))


def along_z(block, d):
    return travel(block, lambda x, z, c, f: (x, z + d, c, f))


def next_shard(block):
    return travel(block, lambda x, z, c, f: (x, z, c, f + 1 - 2 * c))


def swap_core(block):
    return travel(block, lambda x, z, c, f: (x, z, 1 - c, f))


def swap_x(block):
    return travel(block, lambda x, z, c, f: (1 - x, z, c, f))


def halo_rows(block, axis):
    count = lax.axis_size(axis)
    up = [(i, i + 1) for i in range(count - 1)]
    down = [(i + 1, i) for i in range(count - 1)]
    return (
        lax.ppermute(block[:, ROWS - HALF :], axis, up),
        lax.ppermute(block[:, :HALF], axis, down),
    )


def swap_halos(to_low, to_high):
    count = lax.axis_size("ctx")
    up = [(i, i + 1) for i in range(count - 1)]
    down = [(i + 1, i) for i in range(count - 1)]
    return lax.ppermute(to_high, "ctx", up), lax.ppermute(to_low, "ctx", down)


def tables(first_row, lengths):
    half = HD // 2
    frequencies = rope_base ** (-(jnp.arange(half, dtype=F32) * 2.0) / HD)
    positions = first_row - HALF + jnp.arange(EXT, dtype=jnp.int32)
    angles = positions.astype(F32)[:, None] * frequencies[None, :]
    cosine, sine = jnp.cos(angles), jnp.sin(angles)
    cosine = jnp.concatenate([cosine] * 4, axis=1)
    sine = jnp.concatenate([-sine, sine, -sine, sine], axis=1)
    ends = jnp.cumsum(lengths, axis=1)
    doc = jnp.sum((positions[None, :, None] >= ends[:, None, :]).astype(jnp.int32), axis=2)
    query = positions[HALF : HALF + ROWS]
    allowed = (
        (jnp.abs(query[None, :] - positions[:, None]) <= HALF)
        & (positions >= 0)[:, None]
        & (positions < SEQ_LEN)[:, None]
    )[None] & (doc[:, :, None] == doc[:, None, HALF : HALF + ROWS])
    bias = jnp.where(allowed, 0.0, masked_score).astype(F32)
    return cosine, sine, jnp.concatenate([bias, bias], axis=2)


WQKV, WPROJ, WLIFT, WDOWN = [
    pltpu.VMEM((D, WIDE), BF16),
    pltpu.VMEM((D, D), BF16),
    pltpu.VMEM((D, WIDE), BF16),
    pltpu.VMEM((FF, D), BF16),
]
SAVED = [
    ((OWN, D), BF16),
    ((MICRO * EXT, D), BF16),
    ((MICRO * EXT, D), BF16),
    ((MICRO, TILES, EXT, 2 * ROWS), BF16),
    ((OWN, D), BF16),
    ((OWN, D), F32),
    ((OWN, FF), BF16),
    ((OWN, FF), F32),
    ((OWN, FF), F32),
]
STREAM = [pltpu.VMEM((MICRO * EXT, D), BF16)] * 2
GRADS_OUT = [
    ((OWN, D), F32),
    ((OWN, D), BF16),
    ((OWN, 2 * D), F32),
    ((MICRO, HALF, 2 * D), BF16),
    ((MICRO, HALF, 2 * D), BF16),
]


TURN_OUT = [((MICRO, ROWS, D), BF16)] + SAVED + [((OWN, D), BF16)]
BACK_OUT = [((OWN, D), BF16), ((OWN, WIDE), BF16), ((OWN, D), BF16), ((OWN, D), BF16)]


def sems(count):
    return pltpu.SemaphoreType.DMA((count,))


def body(
    inputs, out_grad, doc_lengths, attn_gain, qkv_weight, proj_weight, mlp_gain, lift_weight, down_weight
):
    on_first = lax.axis_index("section") == 0
    flag = on_first.astype(jnp.int32).reshape(1)
    ctx, f = lax.axis_index("ctx"), lax.axis_index("fsdp")
    index = jnp.stack([ctx // 2 % 4, f, ctx % 2]).astype(jnp.int32)
    qkv_shard, lift_shard, proj_shard, down_shard = qkv_weight[0], lift_weight[0], proj_weight[0], down_weight[0]
    own, cotangent = inputs[:, 0], out_grad[:, 0]
    gain_tile = jnp.pad(
        jnp.pad(jnp.stack([attn_gain[0], mlp_gain[0]]), ((0, 0), (0, 64))).reshape(4, 128), ((0, 12), (0, 0))
    )
    edge = ((MICRO, HALF, D), BF16, "a")
    qkv_pack, qkv_half, first_rows, last_rows = call(
        pack_qkv_kernel, "pack_qkv",
        [(index, "s"), (qkv_shard, "a"), (gain_tile, "a"), (own, "a")],
        [((192, 2432), BF16, "a"), ((96, 2432), BF16, "a"), edge, edge],
        [sems(6)], 0, 8,
    )
    low, high = swap_halos(first_rows, last_rows)
    rest, rest_half = call(
        pack_kernel, "pack_rest",
        [(index, "s"), (lift_shard, "a"), (proj_shard, "a"), (down_shard, "a")],
        [((352, WIDE), BF16, "a"), ((176, WIDE), BF16, "a")],
        [sems(14)], 0, 8,
    )
    first = next_shard(qkv_pack)
    second = along_y(qkv_half, 2)
    cosine, sine, bias = tables(ctx * ROWS, doc_lengths[:, 0])
    first, second, rest, rest_half, cosine, sine, bias, low, high = lax.optimization_barrier(
        (first, second, rest, rest_half, cosine, sine, bias, low, high)
    )
    qkv_pieces = first, swap_core(first), second, swap_core(second)
    stream = ((MICRO, ROWS, D), BF16)
    scratch = lambda items: [pltpu.VMEM(s, k) for s, k in items]

    o, gains, wqkv = call(
        forward_attention_kernel, "forward_attention",
        [(index, "s"), (own, "v"), (low, "v"), (high, "v"), (gain_tile, "a"), (cosine, "v"), (sine, "v"), (bias, "v"),
         (qkv_shard, "a"), *[(piece, "a") for piece in qkv_pieces]],
        [((OWN, D), BF16), ((2, D), F32), ((D, WIDE), BF16, "a")],
        [WQKV, pltpu.VMEM((SHARDS, 16, 128), BF16)] + STREAM + scratch(SAVED[:4]) + [sems(9), pltpu.SemaphoreType.DMA(())],
        1_400_000_000, 56,
    )
    rest_first, rest_second, o = lax.optimization_barrier((next_shard(rest), along_y(rest_half, 2), o))
    rest_pieces = rest_first, swap_core(rest_first), rest_second, swap_core(rest_second)
    relay, wproj, wlift, wdown = call(
        forward_mlp_kernel, "forward_mlp",
        [(index, "s"), (own, "v"), (o, "v"), (gains, "v"), (lift_shard, "a"), (proj_shard, "a"), (down_shard, "a"),
         *[(piece, "a") for piece in rest_pieces]],
        [stream, ((D, D), BF16, "a"), ((D, WIDE), BF16, "a"), ((FF, D), BF16, "a")],
        [WPROJ, WLIFT, WDOWN] + scratch([SAVED[5], SAVED[0], SAVED[6]]) + [sems(34)],
        1_800_000_000, 56,
    )
    relayed = lax.ppermute(relay, "section", [(0, 1)])
    other_low, other_high = halo_rows(relayed, "ctx")
    (h3, q, k, v, p, o, h2, m_act, left, right, src, dh2, dq, dkv, to_low, to_high) = call(
        turning_kernel, "layer_turn",
        [(flag, "s"), (own, "v"), (low, "v"), (high, "v"), (relayed, "v"), (other_low, "v"), (other_high, "v"),
         (cotangent, "v"), (gains, "v"), (cosine, "v"), (sine, "v"), (bias, "v"),
         (wqkv, "a"), (wproj, "a"), (wlift, "a"), (wdown, "a")],
        [(*item, "a") for item in TURN_OUT] + GRADS_OUT,
        [WQKV, WPROJ, WLIFT, WDOWN] + STREAM
        + [pltpu.VMEM((MICRO, ROWS, D), BF16), pltpu.VMEM((OWN, WIDE), BF16), pltpu.VMEM((OWN, D), BF16)] + scratch(TURN_OUT) + [sems(15)],
        6_000_000_000, 44,
    )
    from_low, from_high = swap_halos(to_low, to_high)
    (grad_relay,) = call(
        source_kernel, "layer_source",
        [(src, "v"), (gains, "v"), (dh2, "v"), (dq, "v"), (dkv, "v"), (from_low, "v"), (from_high, "v"), (wqkv, "a")],
        [stream],
        [WQKV, pltpu.VMEM((OWN, WIDE), BF16), sems(1)],
        900_000_000,
    )
    incoming = lax.ppermute(grad_relay, "section", [(1, 0)])
    (grad_low, du, gb, b, mlp_gain_grad, dh2, dq, dkv, to_low, to_high) = call(
        back_kernel, "layer_back",
        [(flag, "s"), (incoming, "v"), (cotangent, "v"), (gains, "v"), (cosine, "v"), (sine, "v"),
         (wproj, "a"), (wlift, "a"), (wdown, "a"),
         *[(array, "a") for array in (q, k, v, p, h2, left, right)]],
        [(*item, "a") for item in BACK_OUT] + [((1, D), F32)] + GRADS_OUT,
        [WPROJ, WLIFT, WDOWN, pltpu.VMEM((OWN, D), BF16)]
        + scratch(SAVED[:4] + SAVED[5:6] + SAVED[7:] + BACK_OUT) + [sems(14)],
        3_000_000_000, 40,
    )
    from_low, from_high = swap_halos(to_low, to_high)
    rest_keep, rest_send = call(
        weight_grad_kernel, "weight_grads",
        [(index, "s"), (m_act, "v"), (grad_low, "v"), (b, "v"), (du, "v"), (o, "v"), (gb, "v")],
        [((SHARDS, 192, WIDE), BF16, "a")] * 2,
        [WDOWN, WLIFT, WPROJ, pltpu.VMEM((16, WIDE), BF16), sems(64)],
        1_600_000_000,
    )
    from_low, from_high, rest_send = lax.optimization_barrier((from_low, from_high, rest_send))
    rest_other = swap_core(rest_send)
    in_grad, qkv_keep, qkv_send = call(
        source_grad_kernel, "layer_source_grads",
        [(index, "s"), (src, "v"), (gains, "v"), (dh2, "v"), (dq, "v"), (dkv, "v"), (from_low, "v"),
         (from_high, "v"), (mlp_gain_grad, "v"), (wqkv, "a")],
        [stream, ((SHARDS, 96, 2432), BF16, "a"), ((SHARDS, 96, 2432), BF16, "a")],
        [WQKV, pltpu.VMEM((OWN, WIDE), BF16), WQKV, pltpu.VMEM((SHARDS, 96, 128), BF16), sems(17)],
        1_800_000_000,
    )
    qkv_other = swap_core(qkv_send)

    rest_z = call(
        rest_core_kernel, "rest_core_sum", [(index, "s"), (rest_keep, "v"), (rest_other, "v")],
        [((SHARDS, 48, WIDE), BF16)] * 4, [], 0, 24,
    )
    rest_y = call(
        rest_z_kernel, "rest_z_sum",
        [(index, "s"), (rest_z[0], "v"), *[(along_z(rest_z[d], d), "v") for d in (1, 2, 3)]],
        [((48, WIDE), BF16)] * 4, [], 0, 24,
    )
    qkv_y = call(
        qkv_core_kernel, "qkv_core_sum", [(index, "s"), (qkv_keep, "v"), (qkv_other, "v")],
        [((96, 2432), BF16)] * 4, [], 0, 24,
    )
    qkv_mine, _ = lax.optimization_barrier((qkv_y[0], rest_y[0]))
    qkv_z = call(
        qkv_y_kernel, "qkv_y_sum",
        [(index, "s"), (qkv_mine, "v"), *[(along_y(qkv_y[d], d), "v") for d in (1, 2, 3)]],
        [((48, 1280), BF16)] * 4, [pltpu.VMEM((96, 2432), BF16)], 0, 24,
    )
    (joint,) = call(
        joint_kernel, "joint_sum",
        [(rest_y[0], "v"), *[(along_y(rest_y[d], d), "v") for d in (1, 2, 3)],
         (qkv_z[0], "v"), *[(along_z(qkv_z[d], d), "v") for d in (1, 2, 3)]],
        [((48, 3584), BF16)], [], 0, 24,
    )
    (joint,) = call(
        pair_kernel, "pair_sum", [(joint, "v"), (swap_x(joint), "v")], [((48, 3584), BF16)], [], 0, 24
    )
    mine = [joint] + [along_z(joint, d) for d in (1, 2, 3)]
    theirs = [swap_core(piece) for piece in mine]
    qkv_sum, proj_sum, lift_sum, down_sum, gain_sums = call(
        final_kernel, "final_shard", [(index, "s"), *[(piece, "v") for piece in mine + theirs]],
        [((192, WIDE), F32), ((192, D), F32), ((192, WIDE), F32), ((288, D), F32), ((16, 128), F32)],
        [pltpu.VMEM((2, 192, WIDE), BF16)], 0, 24,
    )
    return (
        h3[None, :, None],
        in_grad[None, :, None],
        gain_sums[0:2].reshape(1, 256)[:, :192],
        qkv_sum[None],
        proj_sum[None],
        gain_sums[2:4].reshape(1, 256)[:, :192],
        lift_sum[None],
        down_sum[None],
    )


def solution(mesh):
    placed = (
        P(None, "fsdp", "ctx", None),
        P(None, "fsdp", "ctx", None),
        P(None, "fsdp", None),
        P("section", "fsdp"),
        P("section", "fsdp", None),
        P("section", "fsdp", None),
        P("section", "fsdp"),
        P("section", "fsdp", None),
        P("section", "fsdp", None),
    )
    return jax.shard_map(
        body,
        mesh=mesh,
        in_specs=placed,
        out_specs=(
            P("section", None, "fsdp", "ctx", None),
            P("section", None, "fsdp", "ctx", None),
            P("section", "fsdp"),
            P("section", "fsdp", None),
            P("section", "fsdp", None),
            P("section", "fsdp"),
            P("section", "fsdp", None),
            P("section", "fsdp", None),
        ),
        check_vma=False,
    )
```

profile of v0, /device:TPU:1, one launch (start us, length us, event | category | flops | bytes accessed | tf_op | source)
XLA Modules:
  0.0 305.0 jit_solution(33571045182585644)
XLA Ops:
  1.5 1.2 copy-done.1
  2.7 1.0 copy-done.3
  3.7 1.4 pack_qkv.1
  5.1 4.9 %collective-permute-start.2 = (bf16[2,64,768]{2,1,0:T(8,128)(2,1)S(1)}, bf16[2,64,768]{2,1,0:T(8,128)(2,1)S(1)}, u32[]{:S(2)}, u32[]{:S(2)}) collective-permute-start(bf16[2,64,768]{2,1,0:T(8,128)(2,1)S(1)} %get-tuple-element.93), channel_id=1, source_target_pairs={{0,4},{4,8},{8,12},{12,16},{16,20},{20,24},{24,28},{28,32},{32,36}... | collective-permute-start | bytes 589832 | tf_op jit(solution)/shard_map/ppermute | solution.py:700
  10.1 1.9 collective-permute-start.3
  12.0 3.0 collective-permute-start.1
  15.8 0.9 reduce_window_sum.14
  17.4 1.3 pack_rest.1
  21.6 4.8 %collective-permute-done.1.second = bf16[96,2432]{1,0:T(8,128)(2,1)} collective-permute-done((bf16[96,2432]{1,0:T(8,128)(2,1)}, bf16[96,2432]{1,0:T(8,128)(2,1)}, u32[]{:S(2)}, u32[]{:S(2)}) %collective-permute-start.1) | collective-permute-done | bytes 466976 | tf_op jit(solution)/shard_map/ppermute | solution.py:663
  26.4 8.4 %collective-permute-done.first = bf16[192,2432]{1,0:T(8,128)(2,1)} collective-permute-done((bf16[192,2432]{1,0:T(8,128)(2,1)S(1)}, bf16[192,2432]{1,0:T(8,128)(2,1)}, u32[]{:S(2)}, u32[]{:S(2)}) %collective-permute-start) | collective-permute-done | bytes 933920 | tf_op jit(solution)/shard_map/ppermute | solution.py:663
  34.9 2.3 collective-permute-start.4
  38.6 1.9 collective-permute-done.7.second_other
  41.3 0.9 copy-done.28
  42.3 10.9 %forward_attention.1 = (bf16[256,768]{1,0:T(8,128)(2,1)}, f32[2,768]{1,0:T(2,128)}, bf16[768,2304]{1,0:T(8,128)(2,1)}) custom-call(s32[3]{0:T(128)} %copy-done.19, bf16[2,128,768]{2,1,0:T(8,128)(2,1)} %bitcast.29, bf16[2,64,768]{2,1,0:T(8,128)(2,1)} %copy-done.14, bf16[2,64,768]{2,1,0:T(8,128)(2,1)} %copy-done.16, bf16[16,128]{1,0:T(8,128)(2,1)} %copy-done.21, ...), custom_call_target="tpu_custom_call" | custom-call | flops 1400000000 | bytes 4666666 | tf_op jit(solution)/shard_map/forward_attention/pallas_call | solution.py:645
  53.2 5.4 %collective-permute-done.5.second = bf16[176,2304]{1,0:T(8,128)(2,1)S(1)} collective-permute-done((bf16[176,2304]{1,0:T(8,128)(2,1)S(1)}, bf16[176,2304]{1,0:T(8,128)(2,1)S(1)}, u32[]{:S(2)}, u32[]{:S(2)}) %collective-permute-start.5) | collective-permute-done | bytes 811040 | tf_op jit(solution)/shard_map/ppermute | solution.py:663
  58.6 13.9 %collective-permute-done.4.first = bf16[352,2304]{1,0:T(8,128)(2,1)S(1)} collective-permute-done((bf16[352,2304]{1,0:T(8,128)(2,1)S(1)}, bf16[352,2304]{1,0:T(8,128)(2,1)S(1)}, u32[]{:S(2)}, u32[]{:S(2)}) %collective-permute-start.4) | collective-permute-done | bytes 1622048 | tf_op jit(solution)/shard_map/ppermute | solution.py:663
  72.5 1.9 collective-permute-start.8
  74.4 4.3 %collective-permute-done.9.second_other = bf16[176,2304]{1,0:T(8,128)(2,1)S(1)} collective-permute-done((bf16[176,2304]{1,0:T(8,128)(2,1)S(1)}, bf16[176,2304]{1,0:T(8,128)(2,1)S(1)}, u32[]{:S(2)}, u32[]{:S(2)}) %collective-permute-start.9) | collective-permute-done | bytes 811040 | tf_op jit(solution)/shard_map/ppermute | solution.py:663
  80.2 9.2 %forward_mlp.1 = (bf16[2,128,768]{2,1,0:T(8,128)(2,1)}, bf16[768,768]{1,0:T(8,128)(2,1)}, bf16[768,2304]{1,0:T(8,128)(2,1)}, bf16[1152,768]{1,0:T(8,128)(2,1)}) custom-call(s32[3]{0:T(128)} %copy-done.19, bf16[2,128,768]{2,1,0:T(8,128)(2,1)} %bitcast.30, bf16[256,768]{1,0:T(8,128)(2,1)} %get-tuple-element.105.o, f32[2,768]{1,0:T(2,128)} %get-tuple-element.106.gains, ...), custom_call_target="tpu_custom_call" | custom-call | flops 1800000000 | bytes 6000000 | tf_op jit(solution)/shard_map/forward_mlp/pallas_call | solution.py:645
  89.3 5.0 %collective-permute-start.10 = (bf16[2,128,768]{2,1,0:T(8,128)(2,1)}, bf16[2,128,768]{2,1,0:T(8,128)(2,1)S(1)}, u32[]{:S(2)}, u32[]{:S(2)}) collective-permute-start(bf16[2,128,768]{2,1,0:T(8,128)(2,1)} %get-tuple-element.109), channel_id=1, source_target_pairs={{0,64},{1,65},{2,66},{3,67},{4,68},{5,69},{6,70},{7,71},{8,72},{9,... | collective-permute-start | bytes 1179656 | tf_op jit(solution)/shard_map/ppermute | solution.py:812
  94.3 8.4 %collective-permute-done.10.other_own = bf16[2,128,768]{2,1,0:T(8,128)(2,1)S(1)} collective-permute-done((bf16[2,128,768]{2,1,0:T(8,128)(2,1)}, bf16[2,128,768]{2,1,0:T(8,128)(2,1)S(1)}, u32[]{:S(2)}, u32[]{:S(2)}) %collective-permute-start.10) | collective-permute-done | bytes 393248 | tf_op jit(solution)/shard_map/ppermute | solution.py:812
  102.8 3.1 %collective-permute-start.12 = (bf16[2,64,768]{2,1,0:T(8,128)(2,1)S(1)}, bf16[2,64,768]{2,1,0:T(8,128)(2,1)S(1)}, u32[]{:S(2)}, u32[]{:S(2)}) collective-permute-start(bf16[2,64,768]{2,1,0:T(8,128)(2,1)S(1)} %get-tuple-element.194), channel_id=1, source_target_pairs={{4,0},{8,4},{12,8},{16,12},{20,16},{24,20},{28,24},{32,28},{36,32}... | collective-permute-start | bytes 589832 | tf_op jit(solution)/shard_map/ppermute | solution.py:692
  105.9 5.5 %collective-permute-start.11 = (bf16[2,64,768]{2,1,0:T(8,128)(2,1)S(1)}, bf16[2,64,768]{2,1,0:T(8,128)(2,1)S(1)}, u32[]{:S(2)}, u32[]{:S(2)}) collective-permute-start(bf16[2,64,768]{2,1,0:T(8,128)(2,1)S(1)} %get-tuple-element.195), channel_id=1, source_target_pairs={{0,4},{4,8},{8,12},{12,16},{16,20},{20,24},{24,28},{28,32},{32,36}... | collective-permute-start | bytes 589832 | tf_op jit(solution)/shard_map/ppermute | solution.py:691
  111.4 1.2 collective-permute-done.12.other_high
  112.6 1.2 collective-permute-done.11.other_low
  113.8 25.0 %layer_turn.1 = (bf16[2,128,768]{2,1,0:T(8,128)(2,1)}, bf16[256,768]{1,0:T(8,128)(2,1)S(1)}, bf16[512,768]{1,0:T(8,128)(2,1)S(1)}, bf16[512,768]{1,0:T(8,128)(2,...) custom-call(s32[1]{0:T(128)} %bitcast.flag_ref, ...), custom_call_target="tpu_custom_call" | custom-call | flops 6000000000 | bytes 20000000 | tf_op jit(solution)/shard_map/layer_turn/pallas_call | solution.py:645
  139.7 4.4 %collective-permute-start.13 = (bf16[2,64,1536]{2,1,0:T(8,128)(2,1)S(1)}, bf16[2,64,1536]{2,1,0:T(8,128)(2,1)S(1)}, u32[]{:S(2)}, u32[]{:S(2)}) collective-permute-start(bf16[2,64,1536]{2,1,0:T(8,128)(2,1)S(1)} %get-tuple-element.119), channel_id=1, source_target_pairs={{0,4},{4,8},{8,12},{12,16},{16,20},{20,24},{24,28},{28,32},{32,36}... | collective-permute-start | bytes 1179656 | tf_op jit(solution)/shard_map/ppermute | solution.py:700
  144.1 1.9 collective-permute-start.14
  146.0 2.8 collective-permute-done.13.from_low
  148.8 4.4 %collective-permute-done.14.from_high = bf16[2,64,1536]{2,1,0:T(8,128)(2,1)S(1)} collective-permute-done((bf16[2,64,1536]{2,1,0:T(8,128)(2,1)S(1)}, bf16[2,64,1536]{2,1,0:T(8,128)(2,1)S(1)}, u32[]{:S(2)}, u32[]{:S(2)}) %collective-permute-start.14) | collective-permute-done | bytes 393248 | tf_op jit(solution)/shard_map/ppermute | solution.py:700
  153.2 1.4 copy-done.7
  154.6 2.2 layer_source.1
  156.8 1.3 collective-permute-start.15
  158.1 8.7 %collective-permute-done.15.incoming = bf16[2,128,768]{2,1,0:T(8,128)(2,1)S(1)} collective-permute-done((bf16[2,128,768]{2,1,0:T(8,128)(2,1)S(1)}, bf16[2,128,768]{2,1,0:T(8,128)(2,1)S(1)}, u32[]{:S(2)}, u32[]{:S(2)}) %collective-permute-start.15) | collective-permute-done | bytes 393248 | tf_op jit(solution)/shard_map/ppermute | solution.py:832
  166.9 13.0 %layer_back.1 = (bf16[256,768]{1,0:T(8,128)(2,1)S(1)}, bf16[256,2304]{1,0:T(8,128)(2,1)S(1)}, bf16[256,768]{1,0:T(8,128)(2,1)S(1)}, bf16[256,768]{1,0:T(8,128)(2...) custom-call(s32[1]{0:T(128)} %bitcast.flag_ref, ...), custom_call_target="tpu_custom_call" | custom-call | flops 3000000000 | bytes 10000000 | tf_op jit(solution)/shard_map/layer_back/pallas_call | solution.py:645
  179.9 6.1 %collective-permute-start.16 = (bf16[2,64,1536]{2,1,0:T(8,128)(2,1)S(1)}, bf16[2,64,1536]{2,1,0:T(8,128)(2,1)S(1)}, u32[]{:S(2)}, u32[]{:S(2)}) collective-permute-start(bf16[2,64,1536]{2,1,0:T(8,128)(2,1)S(1)} %get-tuple-element.131), channel_id=1, source_target_pairs={{0,4},{4,8},{8,12},{12,16},{16,20},{20,24},{24,28},{28,32},{32,36}... | collective-permute-start | bytes 1179656 | tf_op jit(solution)/shard_map/ppermute | solution.py:700
  186.0 2.1 collective-permute-start.17
  188.2 7.0 %weight_grads.1 = (bf16[4,192,2304]{2,1,0:T(8,128)(2,1)S(1)}, bf16[4,192,2304]{2,1,0:T(8,128)(2,1)S(1)}) custom-call(s32[3]{0:T(128)S(1)} %copy-done.20, bf16[256,1152]{1,0:T(8,128)(2,1)S(1)} %copy-done.23, bf16[256,768]{1,0:T(8,128)(2,1)S(1)} %get-tuple-element.134.grad_ref, bf16[256,768]{1,0:T(8,128)(2,1)S(1)} %get-tuple-element.135.b_ref, ...), custom_call_target="tpu_custom_call" | custom-call | flops 1600000000 | bytes 5333333 | tf_op jit(solution)/shard_map/weight_grads/pallas_call | solution.py:645
  195.3 5.0 %layer_source_grads.1 = (bf16[2,128,768]{2,1,0:T(8,128)(2,1)}, bf16[4,96,2432]{2,1,0:T(8,128)(2,1)S(1)}, bf16[4,96,2432]{2,1,0:T(8,128)(2,1)S(1)}) custom-call(s32[3]{0:T(128)S(1)} %copy-done.20, bf16[256,768]{1,0:T(8,128)(2,1)S(1)} %get-tuple-element.115.src, f32[2,768]{1,0:T(2,128)S(1)} %copy-done.18, f32[256,768]{1,0:T(8,128)S(1)} %get-tuple-element.128.dh2, ...), custom_call_target="tpu_custom_call" | custom-call | flops 1800000000 | bytes 6000000 | tf_op jit(solution)/shard_map/layer_source_grads/pallas_call | solution.py:645
  201.5 1.3 rest_core_sum.1
  202.8 2.3 collective-permute-start.19
  205.2 5.3 %collective-permute-start.20 = (bf16[4,48,2304]{2,1,0:T(8,128)(2,1)S(1)}, bf16[4,48,2304]{2,1,0:T(8,128)(2,1)S(1)}, u32[]{:S(2)}, u32[]{:S(2)}) collective-permute-start(bf16[4,48,2304]{2,1,0:T(8,128)(2,1)S(1)} %get-tuple-element.148), channel_id=1, source_target_pairs={{0,16},{1,17},{2,18},{3,19},{4,20},{5,21},{6,22},{7,23},{8,24},{9,... | collective-permute-start | bytes 2654216 | tf_op jit(solution)/shard_map/ppermute | solution.py:663
  210.5 1.0 qkv_core_sum.1
  211.6 2.6 collective-permute-start.27
  214.2 15.0 %collective-permute-done.19.a = bf16[4,48,2304]{2,1,0:T(8,128)(2,1)S(1)} collective-permute-done((bf16[4,48,2304]{2,1,0:T(8,128)(2,1)S(1)}, bf16[4,48,2304]{2,1,0:T(8,128)(2,1)S(1)}, u32[]{:S(2)}, u32[]{:S(2)}) %collective-permute-start.19) | collective-permute-done | bytes 884768 | tf_op jit(solution)/shard_map/ppermute | solution.py:663
  229.2 1.4 collective-permute-start.28
  230.6 18.5 %collective-permute-done.20.b = bf16[4,48,2304]{2,1,0:T(8,128)(2,1)S(1)} collective-permute-done((bf16[4,48,2304]{2,1,0:T(8,128)(2,1)S(1)}, bf16[4,48,2304]{2,1,0:T(8,128)(2,1)S(1)}, u32[]{:S(2)}, u32[]{:S(2)}) %collective-permute-start.20) | collective-permute-done | bytes 884768 | tf_op jit(solution)/shard_map/ppermute | solution.py:663
  249.1 1.0 rest_z_sum.1
  250.1 1.0 qkv_y_sum.1
  251.3 2.6 collective-permute-start.23
  253.9 1.2 collective-permute-start.24
  255.1 3.4 %collective-permute-start.30 = (bf16[48,1280]{1,0:T(8,128)(2,1)S(1)}, bf16[48,1280]{1,0:T(8,128)(2,1)S(1)}, u32[]{:S(2)}, u32[]{:S(2)}) collective-permute-start(bf16[48,1280]{1,0:T(8,128)(2,1)S(1)} %get-tuple-element.163), channel_id=1, source_target_pairs={{0,16},{1,17},{2,18},{3,19},{4,20},{5,21},{6,22},{7,23},{8,24},{9,... | collective-permute-start | bytes 368648 | tf_op jit(solution)/shard_map/ppermute | solution.py:663
  258.5 2.9 collective-permute-done.30.q2
  261.4 0.9 collective-permute-done.31.q3
  262.5 12.0 %collective-permute-start.32 = (bf16[48,3584]{1,0:T(8,128)(2,1)S(1)}, bf16[48,3584]{1,0:T(8,128)(2,1)S(1)}, u32[]{:S(2)}, u32[]{:S(2)}) collective-permute-start(bf16[48,3584]{1,0:T(8,128)(2,1)S(1)} %joint_sum.1.a), channel_id=1, source_target_pairs={{0,32},{1,33},{2,34},{3,35},{4,36},{5,37},{6,38},{7,39},{8,40},{9,... | collective-permute-start | bytes 1032200 | tf_op jit(solution)/shard_map/ppermute | solution.py:663
  274.5 5.8 %collective-permute-done.32.b = bf16[48,3584]{1,0:T(8,128)(2,1)S(1)} collective-permute-done((bf16[48,3584]{1,0:T(8,128)(2,1)S(1)}, bf16[48,3584]{1,0:T(8,128)(2,1)S(1)}, u32[]{:S(2)}, u32[]{:S(2)}) %collective-permute-start.32) | collective-permute-done | bytes 344096 | tf_op jit(solution)/shard_map/ppermute | solution.py:663
  280.8 1.1 collective-permute-start.33
  281.9 4.6 %collective-permute-start.36 = (bf16[48,3584]{1,0:T(8,128)(2,1)S(1)}, bf16[48,3584]{1,0:T(8,128)(2,1)S(1)}, u32[]{:S(2)}, u32[]{:S(2)}) collective-permute-start(bf16[48,3584]{1,0:T(8,128)(2,1)S(1)} %pair_sum.1.refs_0_), channel_id=1, source_target_pairs={{0,4},{1,5},{2,6},{3,7},{4,0},{5,1},{6,2},{7,3},{8,12},{9,13},{10,... | collective-permute-start | bytes 1032200 | tf_op jit(solution)/shard_map/ppermute | solution.py:663
  286.5 8.1 %collective-permute-start.39 = (bf16[48,3584]{1,0:T(8,128)(2,1)S(1)}, bf16[48,3584]{1,0:T(8,128)(2,1)S(1)}, u32[]{:S(2)}, u32[]{:S(2)}) collective-permute-start(bf16[48,3584]{1,0:T(8,128)(2,1)S(1)} %collective-permute-done.35.refs_3_), channel_id=1, source_target_pairs={{0,4},{1,5},{2,6},{3,7},{4,0},{5,1},{6,2},{7,3},{8,12},{9,13},{10,... | collective-permute-start | bytes 1032200 | tf_op jit(solution)/shard_map/ppermute | solution.py:663
  294.6 2.0 collective-permute-start.38
  296.6 1.9 collective-permute-done.33.refs_1_
  298.5 1.7 collective-permute-start.37
  300.2 1.3 collective-permute-done.37.refs_5_
  301.4 3.0 final_shard.1
  (115 shorter events, 12.7 us)
Async XLA Ops:
  1.4 18.2 %copy-start.21 = (bf16[16,128]{1,0:T(8,128)(2,1)}, bf16[16,128]{1,0:T(8,128)(2,1)S(1)}, u32[]{:S(2)}) copy-start(bf16[16,128]{1,0:T(8,128)(2,1)S(1)} %pad.9.gains.gain_tile) | copy-start | bytes 12292
  1.5 18.1 %copy-start.19 = (s32[3]{0:T(128)}, s32[3]{0:T(128)S(1)}, u32[]{:S(2)}) copy-start(s32[3]{0:T(128)S(1)} %pad_add_fusion.index) | copy-start | bytes 40
  3.7 13.7 %copy-start.2 = (bf16[1,192,2304]{2,1,0:T(8,128)(2,1)S(1)}, bf16[1,192,2304]{2,1,0:T(8,128)(2,1)}, u32[]{:S(2)}) copy-start(bf16[1,192,2304]{2,1,0:T(8,128)(2,1)} %param.16) | copy-start | bytes 2654212
  3.7 13.7 %copy-start.6 = (bf16[1,288,768]{2,1,0:T(8,128)(2,1)S(1)}, bf16[1,288,768]{2,1,0:T(8,128)(2,1)}, u32[]{:S(2)}) copy-start(bf16[1,288,768]{2,1,0:T(8,128)(2,1)} %param.17) | copy-start | bytes 1327108
  3.7 13.7 %copy-start.12 = (bf16[1,192,768]{2,1,0:T(8,128)(2,1)S(1)}, bf16[1,192,768]{2,1,0:T(8,128)(2,1)}, u32[]{:S(2)}) copy-start(bf16[1,192,768]{2,1,0:T(8,128)(2,1)} %param.14) | copy-start | bytes 884740
  5.1 16.4 %collective-permute-start.2 = (bf16[2,64,768]{2,1,0:T(8,128)(2,1)S(1)}, bf16[2,64,768]{2,1,0:T(8,128)(2,1)S(1)}, u32[]{:S(2)}, u32[]{:S(2)}) collective-permute-start(bf16[2,64,768]{2,1,0:T(8,128)(2,1)S(1)} %get-tuple-element.93), channel_id=1, source_target_pairs={{0,4},{4,8},{8,12},{12,16},{16,20},{20,24},{24,28},{28,32},{32,36}... | collective-permute-start | bytes 589832 | tf_op jit(solution)/shard_map/ppermute | solution.py:700
  10.1 11.5 %collective-permute-start.3 = (bf16[2,64,768]{2,1,0:T(8,128)(2,1)S(1)}, bf16[2,64,768]{2,1,0:T(8,128)(2,1)S(1)}, u32[]{:S(2)}, u32[]{:S(2)}) collective-permute-start(bf16[2,64,768]{2,1,0:T(8,128)(2,1)S(1)} %get-tuple-element.94), channel_id=1, source_target_pairs={{4,0},{8,4},{12,8},{16,12},{20,16},{24,20},{28,24},{32,28},{36,32}... | collective-permute-start | bytes 589832 | tf_op jit(solution)/shard_map/ppermute | solution.py:700
  12.0 14.4 %collective-permute-start.1 = (bf16[96,2432]{1,0:T(8,128)(2,1)}, bf16[96,2432]{1,0:T(8,128)(2,1)}, u32[]{:S(2)}, u32[]{:S(2)}) collective-permute-start(bf16[96,2432]{1,0:T(8,128)(2,1)} %get-tuple-element.90), channel_id=1, source_target_pairs={{0,2},{1,3},{2,0},{3,1},{4,6},{5,7},{6,4},{7,5},{8,10},{9,11},{10,... | collective-permute-start | bytes 1400840 | tf_op jit(solution)/shard_map/ppermute | solution.py:663
  15.0 19.9 %collective-permute-start = (bf16[192,2432]{1,0:T(8,128)(2,1)S(1)}, bf16[192,2432]{1,0:T(8,128)(2,1)}, u32[]{:S(2)}, u32[]{:S(2)}) collective-permute-start(bf16[192,2432]{1,0:T(8,128)(2,1)S(1)} %get-tuple-element.89), channel_id=1, source_target_pairs={{0,1},{1,2},{2,3},{3,0},{4,7},{5,4},{6,5},{7,6},{8,9},{9,10},{10,1... | collective-permute-start | bytes 2801672 | tf_op jit(solution)/shard_map/ppermute | solution.py:663
  21.6 19.0 %copy-start.14 = (bf16[2,64,768]{2,1,0:T(8,128)(2,1)}, bf16[2,64,768]{2,1,0:T(8,128)(2,1)S(1)}, u32[]{:S(2)}) copy-start(bf16[2,64,768]{2,1,0:T(8,128)(2,1)S(1)} %collective-permute-done.2.low) | copy-start | bytes 589828
  21.6 19.0 %copy-start.16 = (bf16[2,64,768]{2,1,0:T(8,128)(2,1)}, bf16[2,64,768]{2,1,0:T(8,128)(2,1)S(1)}, u32[]{:S(2)}) copy-start(bf16[2,64,768]{2,1,0:T(8,128)(2,1)S(1)} %collective-permute-done.3.high) | copy-start | bytes 589828
  34.9 37.6 %collective-permute-start.4 = (bf16[352,2304]{1,0:T(8,128)(2,1)S(1)}, bf16[352,2304]{1,0:T(8,128)(2,1)S(1)}, u32[]{:S(2)}, u32[]{:S(2)}) collective-permute-start(bf16[352,2304]{1,0:T(8,128)(2,1)S(1)} %get-tuple-element.97), channel_id=1, source_target_pairs={{0,1},{1,2},{2,3},{3,0},{4,7},{5,4},{6,5},{7,6},{8,9},{9,10},{10,1... | collective-permute-start | bytes 4866056 | tf_op jit(solution)/shard_map/ppermute | solution.py:663
  37.2 3.4 %collective-permute-start.6 = (bf16[192,2432]{1,0:T(8,128)(2,1)}, bf16[192,2432]{1,0:T(8,128)(2,1)S(1)}, u32[]{:S(2)}, u32[]{:S(2)}) collective-permute-start(bf16[192,2432]{1,0:T(8,128)(2,1)} %collective-permute-done.first), channel_id=1, source_target_pairs={{0,4},{1,5},{2,6},{3,7},{4,0},{5,1},{6,2},{7,3},{8,12},{9,13},{10,... | collective-permute-start | bytes 2801672 | tf_op jit(solution)/shard_map/ppermute | solution.py:663
  37.2 21.4 %collective-permute-start.5 = (bf16[176,2304]{1,0:T(8,128)(2,1)S(1)}, bf16[176,2304]{1,0:T(8,128)(2,1)S(1)}, u32[]{:S(2)}, u32[]{:S(2)}) collective-permute-start(bf16[176,2304]{1,0:T(8,128)(2,1)S(1)} %get-tuple-element.98), channel_id=1, source_target_pairs={{0,2},{1,3},{2,0},{3,1},{4,6},{5,7},{6,4},{7,5},{8,10},{9,11},{10,... | collective-permute-start | bytes 2433032 | tf_op jit(solution)/shard_map/ppermute | solution.py:663
  37.8 2.7 collective-permute-start.7
  58.6 20.1 %copy-start.29 = (bf16[176,2304]{1,0:T(8,128)(2,1)}, bf16[176,2304]{1,0:T(8,128)(2,1)S(1)}, u32[]{:S(2)}) copy-start(bf16[176,2304]{1,0:T(8,128)(2,1)S(1)} %collective-permute-done.5.second) | copy-start | bytes 2433028
  72.5 6.2 %copy-start.26 = (bf16[352,2304]{1,0:T(8,128)(2,1)}, bf16[352,2304]{1,0:T(8,128)(2,1)S(1)}, u32[]{:S(2)}) copy-start(bf16[352,2304]{1,0:T(8,128)(2,1)S(1)} %collective-permute-done.4.first) | copy-start | bytes 4866052
  72.5 6.2 %collective-permute-start.8 = (bf16[352,2304]{1,0:T(8,128)(2,1)S(1)}, bf16[352,2304]{1,0:T(8,128)(2,1)S(1)}, u32[]{:S(2)}, u32[]{:S(2)}) collective-permute-start(bf16[352,2304]{1,0:T(8,128)(2,1)S(1)} %collective-permute-done.4.first), channel_id=1, source_target_pairs={{0,4},{1,5},{2,6},{3,7},{4,0},{5,1},{6,2},{7,3},{8,12},{9,13},{10,... | collective-permute-start | bytes 4866056 | tf_op jit(solution)/shard_map/ppermute | solution.py:663
  74.4 4.3 %collective-permute-start.9 = (bf16[176,2304]{1,0:T(8,128)(2,1)S(1)}, bf16[176,2304]{1,0:T(8,128)(2,1)S(1)}, u32[]{:S(2)}, u32[]{:S(2)}) collective-permute-start(bf16[176,2304]{1,0:T(8,128)(2,1)S(1)} %collective-permute-done.5.second), channel_id=1, source_target_pairs={{0,4},{1,5},{2,6},{3,7},{4,0},{5,1},{6,2},{7,3},{8,12},{9,13},{10,... | collective-permute-start | bytes 2433032 | tf_op jit(solution)/shard_map/ppermute | solution.py:663
  80.1 33.7 %copy-start.4 = (bf16[2,1,128,768]{3,2,1,0:T(8,128)(2,1)S(1)}, bf16[2,1,128,768]{3,2,1,0:T(8,128)(2,1)}, u32[]{:S(2)}) copy-start(bf16[2,1,128,768]{3,2,1,0:T(8,128)(2,1)} %param.9) | copy-start | bytes 1179652
  80.1 33.7 %copy-start.5 = (f32[2,256,256]{2,1,0:T(8,128)S(1)}, f32[2,256,256]{2,1,0:T(8,128)}, u32[]{:S(2)}) copy-start(f32[2,256,256]{2,1,0:T(8,128)} %pad_maximum_fusion.bias_ref) | copy-start | bytes 1572868
  80.1 33.7 %copy-start.10 = (f32[256,128]{1,0:T(8,128)S(1)}, f32[256,128]{1,0:T(8,128)}, u32[]{:S(2)}) copy-start(f32[256,128]{1,0:T(8,128)} %pad_maximum_fusion.2.sin_ref) | copy-start | bytes 393220
  80.1 33.7 %copy-start.11 = (f32[256,128]{1,0:T(8,128)S(1)}, f32[256,128]{1,0:T(8,128)}, u32[]{:S(2)}) copy-start(f32[256,128]{1,0:T(8,128)} %pad_maximum_fusion.1.cos_ref) | copy-start | bytes 393220
  80.1 33.7 %copy-start.13 = (bf16[2,1,128,768]{3,2,1,0:T(8,128)(2,1)S(1)}, bf16[2,1,128,768]{3,2,1,0:T(8,128)(2,1)}, u32[]{:S(2)}) copy-start(bf16[2,1,128,768]{3,2,1,0:T(8,128)(2,1)} %param.10) | copy-start | bytes 1179652
  80.1 33.7 %copy-start.15 = (bf16[2,64,768]{2,1,0:T(8,128)(2,1)S(1)}, bf16[2,64,768]{2,1,0:T(8,128)(2,1)}, u32[]{:S(2)}) copy-start(bf16[2,64,768]{2,1,0:T(8,128)(2,1)} %copy-done.14) | copy-start | bytes 589828
  80.1 33.7 %copy-start.17 = (bf16[2,64,768]{2,1,0:T(8,128)(2,1)S(1)}, bf16[2,64,768]{2,1,0:T(8,128)(2,1)}, u32[]{:S(2)}) copy-start(bf16[2,64,768]{2,1,0:T(8,128)(2,1)} %copy-done.16) | copy-start | bytes 589828
  80.1 33.7 %copy-start.18 = (f32[2,768]{1,0:T(2,128)S(1)}, f32[2,768]{1,0:T(2,128)}, u32[]{:S(2)}) copy-start(f32[2,768]{1,0:T(2,128)} %get-tuple-element.106.gains) | copy-start | bytes 18436
  89.3 13.4 %collective-permute-start.10 = (bf16[2,128,768]{2,1,0:T(8,128)(2,1)}, bf16[2,128,768]{2,1,0:T(8,128)(2,1)S(1)}, u32[]{:S(2)}, u32[]{:S(2)}) collective-permute-start(bf16[2,128,768]{2,1,0:T(8,128)(2,1)} %get-tuple-element.109), channel_id=1, source_target_pairs={{0,64},{1,65},{2,66},{3,67},{4,68},{5,69},{6,70},{7,71},{8,72},{9,... | collective-permute-start | bytes 1179656 | tf_op jit(solution)/shard_map/ppermute | solution.py:812
  102.8 9.8 %collective-permute-start.12 = (bf16[2,64,768]{2,1,0:T(8,128)(2,1)S(1)}, bf16[2,64,768]{2,1,0:T(8,128)(2,1)S(1)}, u32[]{:S(2)}, u32[]{:S(2)}) collective-permute-start(bf16[2,64,768]{2,1,0:T(8,128)(2,1)S(1)} %get-tuple-element.194), channel_id=1, source_target_pairs={{4,0},{8,4},{12,8},{16,12},{20,16},{24,20},{28,24},{32,28},{36,32}... | collective-permute-start | bytes 589832 | tf_op jit(solution)/shard_map/ppermute | solution.py:692
  105.9 7.9 %collective-permute-start.11 = (bf16[2,64,768]{2,1,0:T(8,128)(2,1)S(1)}, bf16[2,64,768]{2,1,0:T(8,128)(2,1)S(1)}, u32[]{:S(2)}, u32[]{:S(2)}) collective-permute-start(bf16[2,64,768]{2,1,0:T(8,128)(2,1)S(1)} %get-tuple-element.195), channel_id=1, source_target_pairs={{0,4},{4,8},{8,12},{12,16},{16,20},{20,24},{24,28},{28,32},{32,36}... | collective-permute-start | bytes 589832 | tf_op jit(solution)/shard_map/ppermute | solution.py:691
  113.8 39.3 %copy-start = (bf16[768,2304]{1,0:T(8,128)(2,1)S(1)}, bf16[768,2304]{1,0:T(8,128)(2,1)}, u32[]{:S(2)}) copy-start(bf16[768,2304]{1,0:T(8,128)(2,1)} %get-tuple-element.110.qkv_hbm) | copy-start | bytes 10616836
  139.7 17.1 %copy-start.24 = (bf16[256,768]{1,0:T(8,128)(2,1)}, bf16[256,768]{1,0:T(8,128)(2,1)S(1)}, u32[]{:S(2)}) copy-start(bf16[256,768]{1,0:T(8,128)(2,1)S(1)} %get-tuple-element.137.o_ref) | copy-start | bytes 1179652
  139.7 9.1 %collective-permute-start.13 = (bf16[2,64,1536]{2,1,0:T(8,128)(2,1)S(1)}, bf16[2,64,1536]{2,1,0:T(8,128)(2,1)S(1)}, u32[]{:S(2)}, u32[]{:S(2)}) collective-permute-start(bf16[2,64,1536]{2,1,0:T(8,128)(2,1)S(1)} %get-tuple-element.119), channel_id=1, source_target_pairs={{0,4},{4,8},{8,12},{12,16},{16,20},{20,24},{24,28},{28,32},{32,36}... | collective-permute-start | bytes 1179656 | tf_op jit(solution)/shard_map/ppermute | solution.py:700
  144.1 9.1 %collective-permute-start.14 = (bf16[2,64,1536]{2,1,0:T(8,128)(2,1)S(1)}, bf16[2,64,1536]{2,1,0:T(8,128)(2,1)S(1)}, u32[]{:S(2)}, u32[]{:S(2)}) collective-permute-start(bf16[2,64,1536]{2,1,0:T(8,128)(2,1)S(1)} %get-tuple-element.120), channel_id=1, source_target_pairs={{4,0},{8,4},{12,8},{16,12},{20,16},{24,20},{28,24},{32,28},{36,32}... | collective-permute-start | bytes 1179656 | tf_op jit(solution)/shard_map/ppermute | solution.py:700
  154.6 12.3 %copy-start.8 = (bf16[768,768]{1,0:T(8,128)(2,1)S(1)}, bf16[768,768]{1,0:T(8,128)(2,1)}, u32[]{:S(2)}) copy-start(bf16[768,768]{1,0:T(8,128)(2,1)} %get-tuple-element.111.proj_hbm) | copy-start | bytes 3538948
  154.6 12.3 %copy-start.9 = (f32[256,1152]{1,0:T(8,128)S(1)}, f32[256,1152]{1,0:T(8,128)}, u32[]{:S(2)}) copy-start(f32[256,1152]{1,0:T(8,128)} %get-tuple-element.127.right_hbm) | copy-start | bytes 3538948
  156.8 10.0 %collective-permute-start.15 = (bf16[2,128,768]{2,1,0:T(8,128)(2,1)S(1)}, bf16[2,128,768]{2,1,0:T(8,128)(2,1)S(1)}, u32[]{:S(2)}, u32[]{:S(2)}) collective-permute-start(bf16[2,128,768]{2,1,0:T(8,128)(2,1)S(1)} %layer_source.1), channel_id=1, source_target_pairs={{64,0},{65,1},{66,2},{67,3},{68,4},{69,5},{70,6},{71,7},{72,8},{73... | collective-permute-start | bytes 1179656 | tf_op jit(solution)/shard_map/ppermute | solution.py:832
  166.9 21.3 %copy-start.20 = (s32[3]{0:T(128)S(1)}, s32[3]{0:T(128)}, u32[]{:S(2)}) copy-start(s32[3]{0:T(128)} %copy-done.19) | copy-start | bytes 40
  166.9 21.3 %copy-start.23 = (bf16[256,1152]{1,0:T(8,128)(2,1)S(1)}, bf16[256,1152]{1,0:T(8,128)(2,1)}, u32[]{:S(2)}) copy-start(bf16[256,1152]{1,0:T(8,128)(2,1)} %copy-done.22) | copy-start | bytes 1769476
  166.9 21.3 %copy-start.25 = (bf16[256,768]{1,0:T(8,128)(2,1)S(1)}, bf16[256,768]{1,0:T(8,128)(2,1)}, u32[]{:S(2)}) copy-start(bf16[256,768]{1,0:T(8,128)(2,1)} %copy-done.24) | copy-start | bytes 1179652
  179.9 15.3 %collective-permute-start.16 = (bf16[2,64,1536]{2,1,0:T(8,128)(2,1)S(1)}, bf16[2,64,1536]{2,1,0:T(8,128)(2,1)S(1)}, u32[]{:S(2)}, u32[]{:S(2)}) collective-permute-start(bf16[2,64,1536]{2,1,0:T(8,128)(2,1)S(1)} %get-tuple-element.131), channel_id=1, source_target_pairs={{0,4},{4,8},{8,12},{12,16},{16,20},{20,24},{24,28},{28,32},{32,36}... | collective-permute-start | bytes 1179656 | tf_op jit(solution)/shard_map/ppermute | solution.py:700
  186.0 9.2 %collective-permute-start.17 = (bf16[2,64,1536]{2,1,0:T(8,128)(2,1)S(1)}, bf16[2,64,1536]{2,1,0:T(8,128)(2,1)S(1)}, u32[]{:S(2)}, u32[]{:S(2)}) collective-permute-start(bf16[2,64,1536]{2,1,0:T(8,128)(2,1)S(1)} %get-tuple-element.132), channel_id=1, source_target_pairs={{4,0},{8,4},{12,8},{16,12},{20,16},{24,20},{28,24},{32,28},{36,32}... | collective-permute-start | bytes 1179656 | tf_op jit(solution)/shard_map/ppermute | solution.py:700
  195.2 6.3 %collective-permute-start.18 = (bf16[4,192,2304]{2,1,0:T(8,128)(2,1)S(1)}, bf16[4,192,2304]{2,1,0:T(8,128)(2,1)S(1)}, u32[]{:S(2)}, u32[]{:S(2)}) collective-permute-start(bf16[4,192,2304]{2,1,0:T(8,128)(2,1)S(1)} %get-tuple-element.145), channel_id=1, source_target_pairs={{0,4},{1,5},{2,6},{3,7},{4,0},{5,1},{6,2},{7,3},{8,12},{9,13},{10,... | collective-permute-start | bytes 10616840 | tf_op jit(solution)/shard_map/ppermute | solution.py:663
  200.2 10.2 %collective-permute-start.25 = (bf16[4,96,2432]{2,1,0:T(8,128)(2,1)S(1)}, bf16[4,96,2432]{2,1,0:T(8,128)(2,1)S(1)}, u32[]{:S(2)}, u32[]{:S(2)}) collective-permute-start(bf16[4,96,2432]{2,1,0:T(8,128)(2,1)S(1)} %get-tuple-element.155), channel_id=1, source_target_pairs={{0,4},{1,5},{2,6},{3,7},{4,0},{5,1},{6,2},{7,3},{8,12},{9,13},{10,... | collective-permute-start | bytes 5603336 | tf_op jit(solution)/shard_map/ppermute | solution.py:663
  202.8 26.3 %collective-permute-start.19 = (bf16[4,48,2304]{2,1,0:T(8,128)(2,1)S(1)}, bf16[4,48,2304]{2,1,0:T(8,128)(2,1)S(1)}, u32[]{:S(2)}, u32[]{:S(2)}) collective-permute-start(bf16[4,48,2304]{2,1,0:T(8,128)(2,1)S(1)} %get-tuple-element.147), channel_id=1, source_target_pairs={{0,8},{1,9},{2,10},{3,11},{4,12},{5,13},{6,14},{7,15},{8,16},{9,17... | collective-permute-start | bytes 2654216 | tf_op jit(solution)/shard_map/ppermute | solution.py:663
  205.2 43.9 %collective-permute-start.20 = (bf16[4,48,2304]{2,1,0:T(8,128)(2,1)S(1)}, bf16[4,48,2304]{2,1,0:T(8,128)(2,1)S(1)}, u32[]{:S(2)}, u32[]{:S(2)}) collective-permute-start(bf16[4,48,2304]{2,1,0:T(8,128)(2,1)S(1)} %get-tuple-element.148), channel_id=1, source_target_pairs={{0,16},{1,17},{2,18},{3,19},{4,20},{5,21},{6,22},{7,23},{8,24},{9,... | collective-permute-start | bytes 2654216 | tf_op jit(solution)/shard_map/ppermute | solution.py:663
  210.5 38.6 %collective-permute-start.21 = (bf16[4,48,2304]{2,1,0:T(8,128)(2,1)S(1)}, bf16[4,48,2304]{2,1,0:T(8,128)(2,1)S(1)}, u32[]{:S(2)}, u32[]{:S(2)}) collective-permute-start(bf16[4,48,2304]{2,1,0:T(8,128)(2,1)S(1)} %get-tuple-element.149), channel_id=1, source_target_pairs={{0,24},{1,25},{2,26},{3,27},{4,28},{5,29},{6,30},{7,31},{8,0},{9,1... | collective-permute-start | bytes 2654216 | tf_op jit(solution)/shard_map/ppermute | solution.py:663
  211.5 38.6 %collective-permute-start.26 = (bf16[96,2432]{1,0:T(8,128)(2,1)S(1)}, bf16[96,2432]{1,0:T(8,128)(2,1)S(1)}, u32[]{:S(2)}, u32[]{:S(2)}) collective-permute-start(bf16[96,2432]{1,0:T(8,128)(2,1)S(1)} %get-tuple-element.158), channel_id=1, source_target_pairs={{0,1},{1,2},{2,3},{3,0},{4,5},{5,6},{6,7},{7,4},{8,9},{9,10},{10,1... | collective-permute-start | bytes 1400840 | tf_op jit(solution)/shard_map/ppermute | solution.py:663
  211.6 38.5 %collective-permute-start.27 = (bf16[96,2432]{1,0:T(8,128)(2,1)S(1)}, bf16[96,2432]{1,0:T(8,128)(2,1)S(1)}, u32[]{:S(2)}, u32[]{:S(2)}) collective-permute-start(bf16[96,2432]{1,0:T(8,128)(2,1)S(1)} %get-tuple-element.159), channel_id=1, source_target_pairs={{0,2},{1,3},{2,0},{3,1},{4,6},{5,7},{6,4},{7,5},{8,10},{9,11},{10,... | collective-permute-start | bytes 1400840 | tf_op jit(solution)/shard_map/ppermute | solution.py:663
  229.2 20.9 %collective-permute-start.28 = (bf16[96,2432]{1,0:T(8,128)(2,1)S(1)}, bf16[96,2432]{1,0:T(8,128)(2,1)S(1)}, u32[]{:S(2)}, u32[]{:S(2)}) collective-permute-start(bf16[96,2432]{1,0:T(8,128)(2,1)S(1)} %get-tuple-element.160), channel_id=1, source_target_pairs={{0,3},{1,0},{2,1},{3,2},{4,7},{5,4},{6,5},{7,6},{8,11},{9,8},{10,9... | collective-permute-start | bytes 1400840 | tf_op jit(solution)/shard_map/ppermute | solution.py:663
  251.1 7.4 %collective-permute-start.29 = (bf16[48,1280]{1,0:T(8,128)(2,1)S(1)}, bf16[48,1280]{1,0:T(8,128)(2,1)S(1)}, u32[]{:S(2)}, u32[]{:S(2)}) collective-permute-start(bf16[48,1280]{1,0:T(8,128)(2,1)S(1)} %get-tuple-element.162), channel_id=1, source_target_pairs={{0,8},{1,9},{2,10},{3,11},{4,12},{5,13},{6,14},{7,15},{8,16},{9,17... | collective-permute-start | bytes 368648 | tf_op jit(solution)/shard_map/ppermute | solution.py:663
  251.2 11.1 %collective-permute-start.22 = (bf16[48,2304]{1,0:T(8,128)(2,1)S(1)}, bf16[48,2304]{1,0:T(8,128)(2,1)S(1)}, u32[]{:S(2)}, u32[]{:S(2)}) collective-permute-start(bf16[48,2304]{1,0:T(8,128)(2,1)S(1)} %get-tuple-element.151), channel_id=1, source_target_pairs={{0,1},{1,2},{2,3},{3,0},{4,5},{5,6},{6,7},{7,4},{8,9},{9,10},{10,1... | collective-permute-start | bytes 663560 | tf_op jit(solution)/shard_map/ppermute | solution.py:663
  251.3 11.0 %collective-permute-start.23 = (bf16[48,2304]{1,0:T(8,128)(2,1)S(1)}, bf16[48,2304]{1,0:T(8,128)(2,1)S(1)}, u32[]{:S(2)}, u32[]{:S(2)}) collective-permute-start(bf16[48,2304]{1,0:T(8,128)(2,1)S(1)} %get-tuple-element.152), channel_id=1, source_target_pairs={{0,2},{1,3},{2,0},{3,1},{4,6},{5,7},{6,4},{7,5},{8,10},{9,11},{10,... | collective-permute-start | bytes 663560 | tf_op jit(solution)/shard_map/ppermute | solution.py:663
  253.9 8.4 %collective-permute-start.24 = (bf16[48,2304]{1,0:T(8,128)(2,1)S(1)}, bf16[48,2304]{1,0:T(8,128)(2,1)S(1)}, u32[]{:S(2)}, u32[]{:S(2)}) collective-permute-start(bf16[48,2304]{1,0:T(8,128)(2,1)S(1)} %get-tuple-element.153), channel_id=1, source_target_pairs={{0,3},{1,0},{2,1},{3,2},{4,7},{5,4},{6,5},{7,6},{8,11},{9,8},{10,9... | collective-permute-start | bytes 663560 | tf_op jit(solution)/shard_map/ppermute | solution.py:663
  255.1 6.3 %collective-permute-start.30 = (bf16[48,1280]{1,0:T(8,128)(2,1)S(1)}, bf16[48,1280]{1,0:T(8,128)(2,1)S(1)}, u32[]{:S(2)}, u32[]{:S(2)}) collective-permute-start(bf16[48,1280]{1,0:T(8,128)(2,1)S(1)} %get-tuple-element.163), channel_id=1, source_target_pairs={{0,16},{1,17},{2,18},{3,19},{4,20},{5,21},{6,22},{7,23},{8,24},{9,... | collective-permute-start | bytes 368648 | tf_op jit(solution)/shard_map/ppermute | solution.py:663
  258.5 3.8 %collective-permute-start.31 = (bf16[48,1280]{1,0:T(8,128)(2,1)S(1)}, bf16[48,1280]{1,0:T(8,128)(2,1)S(1)}, u32[]{:S(2)}, u32[]{:S(2)}) collective-permute-start(bf16[48,1280]{1,0:T(8,128)(2,1)S(1)} %get-tuple-element.164), channel_id=1, source_target_pairs={{0,24},{1,25},{2,26},{3,27},{4,28},{5,29},{6,30},{7,31},{8,0},{9,1... | collective-permute-start | bytes 368648 | tf_op jit(solution)/shard_map/ppermute | solution.py:663
  262.5 17.8 %collective-permute-start.32 = (bf16[48,3584]{1,0:T(8,128)(2,1)S(1)}, bf16[48,3584]{1,0:T(8,128)(2,1)S(1)}, u32[]{:S(2)}, u32[]{:S(2)}) collective-permute-start(bf16[48,3584]{1,0:T(8,128)(2,1)S(1)} %joint_sum.1.a), channel_id=1, source_target_pairs={{0,32},{1,33},{2,34},{3,35},{4,36},{5,37},{6,38},{7,39},{8,40},{9,... | collective-permute-start | bytes 1032200 | tf_op jit(solution)/shard_map/ppermute | solution.py:663
  280.4 6.2 %collective-permute-start.35 = (bf16[48,3584]{1,0:T(8,128)(2,1)S(1)}, bf16[48,3584]{1,0:T(8,128)(2,1)S(1)}, u32[]{:S(2)}, u32[]{:S(2)}) collective-permute-start(bf16[48,3584]{1,0:T(8,128)(2,1)S(1)} %pair_sum.1.refs_0_), channel_id=1, source_target_pairs={{0,24},{1,25},{2,26},{3,27},{4,28},{5,29},{6,30},{7,31},{8,0},{9,1... | collective-permute-start | bytes 1032200 | tf_op jit(solution)/shard_map/ppermute | solution.py:663
  280.8 13.8 %collective-permute-start.34 = (bf16[48,3584]{1,0:T(8,128)(2,1)S(1)}, bf16[48,3584]{1,0:T(8,128)(2,1)S(1)}, u32[]{:S(2)}, u32[]{:S(2)}) collective-permute-start(bf16[48,3584]{1,0:T(8,128)(2,1)S(1)} %pair_sum.1.refs_0_), channel_id=1, source_target_pairs={{0,16},{1,17},{2,18},{3,19},{4,20},{5,21},{6,22},{7,23},{8,24},{9,... | collective-permute-start | bytes 1032200 | tf_op jit(solution)/shard_map/ppermute | solution.py:663
  280.8 17.7 %collective-permute-start.33 = (bf16[48,3584]{1,0:T(8,128)(2,1)S(1)}, bf16[48,3584]{1,0:T(8,128)(2,1)S(1)}, u32[]{:S(2)}, u32[]{:S(2)}) collective-permute-start(bf16[48,3584]{1,0:T(8,128)(2,1)S(1)} %pair_sum.1.refs_0_), channel_id=1, source_target_pairs={{0,8},{1,9},{2,10},{3,11},{4,12},{5,13},{6,14},{7,15},{8,16},{9,17... | collective-permute-start | bytes 1032200 | tf_op jit(solution)/shard_map/ppermute | solution.py:663
  281.9 18.3 %collective-permute-start.36 = (bf16[48,3584]{1,0:T(8,128)(2,1)S(1)}, bf16[48,3584]{1,0:T(8,128)(2,1)S(1)}, u32[]{:S(2)}, u32[]{:S(2)}) collective-permute-start(bf16[48,3584]{1,0:T(8,128)(2,1)S(1)} %pair_sum.1.refs_0_), channel_id=1, source_target_pairs={{0,4},{1,5},{2,6},{3,7},{4,0},{5,1},{6,2},{7,3},{8,12},{9,13},{10,... | collective-permute-start | bytes 1032200 | tf_op jit(solution)/shard_map/ppermute | solution.py:663
  286.5 13.6 %collective-permute-start.39 = (bf16[48,3584]{1,0:T(8,128)(2,1)S(1)}, bf16[48,3584]{1,0:T(8,128)(2,1)S(1)}, u32[]{:S(2)}, u32[]{:S(2)}) collective-permute-start(bf16[48,3584]{1,0:T(8,128)(2,1)S(1)} %collective-permute-done.35.refs_3_), channel_id=1, source_target_pairs={{0,4},{1,5},{2,6},{3,7},{4,0},{5,1},{6,2},{7,3},{8,12},{9,13},{10,... | collective-permute-start | bytes 1032200 | tf_op jit(solution)/shard_map/ppermute | solution.py:663
  294.6 5.6 %collective-permute-start.38 = (bf16[48,3584]{1,0:T(8,128)(2,1)S(1)}, bf16[48,3584]{1,0:T(8,128)(2,1)S(1)}, u32[]{:S(2)}, u32[]{:S(2)}) collective-permute-start(bf16[48,3584]{1,0:T(8,128)(2,1)S(1)} %collective-permute-done.34.refs_2_), channel_id=1, source_target_pairs={{0,4},{1,5},{2,6},{3,7},{4,0},{5,1},{6,2},{7,3},{8,12},{9,13},{10,... | collective-permute-start | bytes 1032200 | tf_op jit(solution)/shard_map/ppermute | solution.py:663
  298.5 2.9 collective-permute-start.37
  (8 other events, 8.4 us)
where the time goes:
time: 307 us; the launch traced here: 305 us
  waiting for transfers between devices  112 us (36%)
  starting transfers between devices  95.3 us (31%)
  Pallas kernels  82.6 us (27%)
  local copies, waits for them, and re-layouts  8.37 us (3%)
  other arithmetic  5.07 us (2%)
    ppermute x30, waiting for transfers between devices, travel(): return lax.ppermute(block, ('ctx', 'fsdp'), pairs)  85.7 us
    pallas_call x16, Pallas kernels, call(): pl.pallas_call(kernel, name=name, out_shape=[jax.ShapeDtypeStruct(out[0],...  82.6 us
    ppermute x30, starting transfers between devices, travel(): return lax.ppermute(block, ('ctx', 'fsdp'), pairs)  59.1 us
    ppermute x6, starting transfers between devices, swap_halos(): return (lax.ppermute(to_high, 'ctx', up), lax.ppermute(to_low, 'ctx', down))  21.4 us
    ppermute x1, waiting for transfers between devices, body(): incoming = lax.ppermute(grad_relay, 'section', [(1, 0)])  8.73 us
    ppermute x1, waiting for transfers between devices, body(): relayed = lax.ppermute(relay, 'section', [(0, 1)])  8.4 us
    unnamed x64, local copies, waits for them, and re-layouts  7.61 us
    ppermute x6, waiting for transfers between devices, swap_halos(): return (lax.ppermute(to_high, 'ctx', up), lax.ppermute(to_low, 'ctx', down))  7.18 us
  transfers between devices with their start and end apart: 40, of which 21 were waited for; matrix products, arithmetic and copies ran while one was open for 1% of the time, Pallas kernels for 9%

commit v1 on v0

--- a/solution.py
+++ b/solution.py
@@ -19,7 +19,6 @@
 OWN = MICRO * ROWS
 SHARDS = 4
 TILES = D // 128
-GROUP = 2
 norm_eps = 1e-05
 rope_base = 10000.0
 masked_score = -1e30
@@ -124,12 +123,12 @@
     return pl.ds(pl.multiple_of(start, unit), size)
 
 
-def by_tiles(unit):
+def by_tiles(unit, group):
     def step(i):
-        for j in range(GROUP):
-            unit(i * GROUP + j)
-
-    repeat(TILES // GROUP, step)
+        for j in range(group):
+            unit(i * group + j)
+
+    repeat(TILES // group, step)
 
 
 def norm_rows(source, gain, target):
@@ -174,7 +173,7 @@
             attended = mm_tn(probs, v_ref[pl.ds(m * EXT, EXT), cols])
             o_ref[pl.ds(m * ROWS, ROWS), cols] = join_heads(attended).astype(BF16)
 
-    by_tiles(unit)
+    by_tiles(unit, 3)
 
 
 def forward_mlp(own, o_ref, wproj, mlp_gain, wlift, wdown, h2_ref, b_ref, m_ref, left_ref, right_ref, h3_ref, waits):
@@ -253,7 +252,7 @@
     repeat(3, attended)
 
 
-def backward_attention(q_ref, k_ref, v_ref, p_ref, do_ref, cos_ref, sin_ref, dq_ref, dkv_ref, low_ref, high_ref):
+def backward_attention(q_ref, k_ref, v_ref, p_ref, do_ref, cos_ref, sin_ref, dq_ref, dkv_ref, low_ref, high_ref, group):
     cosine, sine = cos_ref[...], sin_ref[...]
     cos_own, sin_own = cosine[HALF : HALF + ROWS], sine[HALF : HALF + ROWS]
 
@@ -278,7 +277,7 @@
                 dkv_ref[rows, where] = grad[HALF : HALF + ROWS]
                 high_ref[m, :, where] = grad[HALF + ROWS :].astype(BF16)
 
-    by_tiles(unit)
+    by_tiles(unit, group)
 
 
 def place_shards(index, own, first, first_other, second, second_other, put):
@@ -375,21 +374,11 @@
     out.wait()
 
 
-def forward_mlp_kernel(index, own, o, gains, lift, proj, down, first, first_other, second, second_other,
-                       h3_ref, whole_proj, whole_lift, whole_down, wproj, wlift, wdown, h2, b, m_out, sems):
-    waits = {"proj": [], "lift": [], "down": []}
-    count = [0]
-
-    def go(name, src, dst):
-        copy = pltpu.make_async_copy(src, dst, sems.at[count[0]])
-        copy.start()
-        count[0] += 1
-        waits[name].append(copy)
-
+def place_rest(index, lift, proj, down, pieces, wlift, wproj, wdown, go):
     f = index[1]
+    rows = lambda at, size: pl.ds(pl.multiple_of(at, 16), size)
 
     def put(piece, s, half):
-        rows = lambda at, size: pl.ds(pl.multiple_of(at, 16), size)
         if piece is None:
             go("proj", proj, wproj.at[rows(f * 192, 192)])
             go("lift", lift, wlift.at[rows(f * 192, 192)])
@@ -403,18 +392,36 @@
             go("proj", piece.at[pl.ds(96 * n, 32 * n), cols], wproj.at[rows(s * 192 + b * 64 + h * 32, 32 * n)])
             go("down", piece.at[pl.ds(128 * n, 48 * n), cols], wdown.at[rows(s * 288 + b * 96 + h * 48, 48 * n)])
 
-    place_shards(index, None, first, first_other, second, second_other, put)
-    outs = []
-    for name, buffer, whole in (("proj", wproj, whole_proj), ("lift", wlift, whole_lift), ("down", wdown, whole_down)):
-        finish(waits, name)
-        copy = pltpu.make_async_copy(buffer, whole, sems.at[count[0]])
+    place_shards(index, None, *pieces, put)
+
+
+def starter(sems, waits):
+    count = [0]
+
+    def go(name, src, dst):
+        copy = pltpu.make_async_copy(src, dst, sems.at[count[0]])
         copy.start()
         count[0] += 1
-        outs.append(copy)
-        waits[name] = []
+        waits.setdefault(name, []).append(copy)
+
+    return go
+
+
+def forward_mlp_kernel(index, own, o, gains, lift, proj, down, first, first_other, second, second_other,
+                       h3_ref, wproj, wlift, wdown, h2, b, m_out, sems):
+    waits = {}
+    pieces = (first, first_other, second, second_other)
+    place_rest(index, lift, proj, down, pieces, wlift, wproj, wdown, starter(sems, waits))
     forward_mlp(own, o, wproj, gains[1:2], wlift, wdown, h2, b, m_out, None, None, h3_ref, waits)
-    for copy in outs:
-        copy.wait()
+
+
+def assemble_kernel(index, lift, proj, down, first, first_other, second, second_other, _,
+                    whole_lift, whole_proj, whole_down, sems):
+    waits = {}
+    pieces = (first, first_other, second, second_other)
+    place_rest(index, lift, proj, down, pieces, whole_lift, whole_proj, whole_down, starter(sems, waits))
+    for name in waits:
+        finish(waits, name)
 
 
 def start_all(pairs, sems, first):
@@ -447,7 +454,7 @@
     for m in range(MICRO):
         grad[pl.ds(m * ROWS, ROWS), :] = cotangent[m]
     backward_mlp(grad, h2, gains[1:2], wproj, wlift, wdown, left, right, du, spare, do, dh2_ref, None, None)
-    backward_attention(q, k, v, p, do, cos_ref, sin_ref, dq, dkv, to_low, to_high)
+    backward_attention(q, k, v, p, do, cos_ref, sin_ref, dq, dkv, to_low, to_high, 3)
     for copy in outs:
         copy.wait()
 
@@ -472,7 +479,7 @@
     outs = start_all(zip((grad_ref, du, gb_ref, b_ref), kept), sems, 10)
     for copy in late:
         copy.wait()
-    backward_attention(q, k, v, p, do, cos_ref, sin_ref, dq, dkv, to_low, to_high)
+    backward_attention(q, k, v, p, do, cos_ref, sin_ref, dq, dkv, to_low, to_high, 6)
     for copy in outs:
         copy.wait()
 
@@ -599,8 +606,12 @@
         out[...] = add_up([keep[f], other[f]])
 
 
-def qkv_y_kernel(index, own, a, b, c, out_0, out_1, out_2, out_3, total):
-    total[...] = add_up([own[...], a[...], b[...], c[...]])
+def partial_kernel(a, b, out):
+    out[...] = a[...].astype(F32) + b[...].astype(F32)
+
+
+def qkv_y_kernel(index, some, b, c, out_0, out_1, out_2, out_3, total):
+    total[...] = add_up([some[...], b[...], c[...]])
     for d, out in enumerate((out_0, out_1, out_2, out_3)):
         z = lax.rem(index[0] + d, 4)
         rows = pl.ds(pl.multiple_of(lax.div(z, 2) * 48, 16), 48)
@@ -772,18 +783,19 @@
         pack_qkv_kernel, "pack_qkv",
         [(index, "s"), (qkv_shard, "a"), (gain_tile, "a"), (own, "a")],
         [((192, 2432), BF16, "a"), ((96, 2432), BF16, "a"), edge, edge],
-        [sems(6)], 0, 8,
-    )
-    low, high = swap_halos(first_rows, last_rows)
+        [sems(6)], 0, 56,
+    )
     rest, rest_half = call(
         pack_kernel, "pack_rest",
         [(index, "s"), (lift_shard, "a"), (proj_shard, "a"), (down_shard, "a")],
         [((352, WIDE), BF16, "a"), ((176, WIDE), BF16, "a")],
-        [sems(14)], 0, 8,
+        [sems(14)], 0, 56,
     )
     first = next_shard(qkv_pack)
     second = along_y(qkv_half, 2)
     cosine, sine, bias = tables(ctx * ROWS, doc_lengths[:, 0])
+    first_rows, last_rows, cosine = lax.optimization_barrier((first_rows, last_rows, cosine))
+    low, high = swap_halos(first_rows, last_rows)
     first, second, rest, rest_half, cosine, sine, bias, low, high = lax.optimization_barrier(
         (first, second, rest, rest_half, cosine, sine, bias, low, high)
     )
@@ -797,17 +809,23 @@
          (qkv_shard, "a"), *[(piece, "a") for piece in qkv_pieces]],
         [((OWN, D), BF16), ((2, D), F32), ((D, WIDE), BF16, "a")],
         [WQKV, pltpu.VMEM((SHARDS, 16, 128), BF16)] + STREAM + scratch(SAVED[:4]) + [sems(9), pltpu.SemaphoreType.DMA(())],
-        1_400_000_000, 56,
+        1_400_000_000,
     )
     rest_first, rest_second, o = lax.optimization_barrier((next_shard(rest), along_y(rest_half, 2), o))
     rest_pieces = rest_first, swap_core(rest_first), rest_second, swap_core(rest_second)
-    relay, wproj, wlift, wdown = call(
+    rest_parts = [(part, "a") for part in (lift_shard, proj_shard, down_shard, *rest_pieces)]
+    (relay,) = call(
         forward_mlp_kernel, "forward_mlp",
-        [(index, "s"), (own, "v"), (o, "v"), (gains, "v"), (lift_shard, "a"), (proj_shard, "a"), (down_shard, "a"),
-         *[(piece, "a") for piece in rest_pieces]],
-        [stream, ((D, D), BF16, "a"), ((D, WIDE), BF16, "a"), ((FF, D), BF16, "a")],
-        [WPROJ, WLIFT, WDOWN] + scratch([SAVED[5], SAVED[0], SAVED[6]]) + [sems(34)],
-        1_800_000_000, 56,
+        [(index, "s"), (own, "v"), (o, "v"), (gains, "v"), *rest_parts],
+        [stream],
+        [WPROJ, WLIFT, WDOWN] + scratch([SAVED[5], SAVED[0], SAVED[6]]) + [sems(31)],
+        1_800_000_000,
+    )
+    wlift, wproj, wdown = call(
+        assemble_kernel, "assemble_weights",
+        [(index, "s"), *rest_parts, (relay, "a")],
+        [((D, WIDE), BF16, "a"), ((D, D), BF16, "a"), ((FF, D), BF16, "a")],
+        [sems(31)], 1_800_000_000, 56,
     )
     relayed = lax.ppermute(relay, "section", [(0, 1)])
     other_low, other_high = halo_rows(relayed, "ctx")
@@ -864,19 +882,25 @@
         rest_core_kernel, "rest_core_sum", [(index, "s"), (rest_keep, "v"), (rest_other, "v")],
         [((SHARDS, 48, WIDE), BF16)] * 4, [], 0, 24,
     )
-    rest_y = call(
-        rest_z_kernel, "rest_z_sum",
-        [(index, "s"), (rest_z[0], "v"), *[(along_z(rest_z[d], d), "v") for d in (1, 2, 3)]],
-        [((48, WIDE), BF16)] * 4, [], 0, 24,
-    )
+    qkv_keep, _ = lax.optimization_barrier((qkv_keep, rest_z[0]))
     qkv_y = call(
         qkv_core_kernel, "qkv_core_sum", [(index, "s"), (qkv_keep, "v"), (qkv_other, "v")],
         [((96, 2432), BF16)] * 4, [], 0, 24,
     )
-    qkv_mine, _ = lax.optimization_barrier((qkv_y[0], rest_y[0]))
+    (some,) = call(
+        partial_kernel, "qkv_y_first", [(qkv_y[0], "v"), (along_y(qkv_y[1], 1), "v")],
+        [((96, 2432), F32)], [], 0, 24,
+    )
+    rest_mine, some = lax.optimization_barrier((rest_z[0], some))
+    rest_y = call(
+        rest_z_kernel, "rest_z_sum",
+        [(index, "s"), (rest_mine, "v"), *[(along_z(rest_z[d], d), "v") for d in (1, 2, 3)]],
+        [((48, WIDE), BF16)] * 4, [], 0, 24,
+    )
+    some, _ = lax.optimization_barrier((some, rest_y[0]))
     qkv_z = call(
         qkv_y_kernel, "qkv_y_sum",
-        [(index, "s"), (qkv_mine, "v"), *[(along_y(qkv_y[d], d), "v") for d in (1, 2, 3)]],
+        [(index, "s"), (some, "v"), *[(along_y(qkv_y[d], d), "v") for d in (2, 3)]],
         [((48, 1280), BF16)] * 4, [pltpu.VMEM((96, 2432), BF16)], 0, 24,
     )
     (joint,) = call(

time: 307 us -> 606 us (1.97)
  Pallas kernels: 82.6 us -> 400 us
  waiting for transfers between devices: 112 us -> 101 us
  starting transfers between devices: 95.3 us -> 86.2 us
    pallas_call x16 -> x18, Pallas kernels: 82.6 us -> 400 us  [call(): pl.pallas_call(kernel, name=name, out_shape=[jax.ShapeDtypeStruct(out[0],...]
    ppermute x30, waiting for transfers between devices: 85.7 us -> 76.8 us  [travel(): return lax.ppermute(block, ('ctx', 'fsdp'), pairs)]
  transfers between devices with their start and end apart: 40 -> 40, of which waited for: 21 -> 22; matrix products, arithmetic and copies ran while one was open for 1% -> 0% of each run, Pallas kernels for 9% -> 50%
where the time goes in v1:
time: 606 us; the launch traced here: 598 us
  Pallas kernels  400 us (66%)
  waiting for transfers between devices  101 us (17%)
  starting transfers between devices  86.2 us (14%)
    pallas_call x18, Pallas kernels, call(): pl.pallas_call(kernel, name=name, out_shape=[jax.ShapeDtypeStruct(out[0],...  400 us
    ppermute x30, waiting for transfers between devices, travel(): return lax.ppermute(block, ('ctx', 'fsdp'), pairs)  76.8 us
    ppermute x30, starting transfers between devices, travel(): return lax.ppermute(block, ('ctx', 'fsdp'), pairs)  53.6 us
    ppermute x6, starting transfers between devices, swap_halos(): return (lax.ppermute(to_high, 'ctx', up), lax.ppermute(to_low, 'ctx', down))  16.7 us
  transfers between devices with their start and end apart: 40, of which 22 were waited for; matrix products, arithmetic and copies ran while one was open for 0% of the time, Pallas kernels for 50%

profile of v1, /device:TPU:1, one launch (start us, length us, event | category | flops | bytes accessed | tf_op | source)
XLA Modules:
  0.0 598.2 jit_solution(2926824815497531586)
XLA Ops:
  2.7 54.2 %pack_qkv.1 = (bf16[192,2432]{1,0:T(8,128)(2,1)}, bf16[96,2432]{1,0:T(8,128)(2,1)}, bf16[2,64,768]{2,1,0:T(8,128)(2,1)}, bf16[2,64,768]{2,1,0:T(8,128)(2,1)}) custom-call(s32[3]{0:T(128)} %pad_add_fusion.index, bf16[192,2304]{1,0:T(8,128)(2,1)} %bitcast.35, bf16[16,128]{1,0:T(8,128)(2,1)} %pad.9.gains.gain_tile, bf16[2,128,768]{2,1,0:T(8,128)(2,1)} %bitcast.31), custom_call_target="tpu_custom_call" | custom-call | tf_op jit(solution)/shard_map/pack_qkv/pallas_call | solution.py:656
  56.9 3.6 collective-permute-start
  61.1 0.8 pad_maximum_fusion.1.cos_ref
  61.9 2.9 collective-permute-start.2
  64.8 1.9 collective-permute-start.3
  66.8 2.7 collective-permute-start.1
  69.9 75.6 %pack_rest.1 = (bf16[352,2304]{1,0:T(8,128)(2,1)}, bf16[176,2304]{1,0:T(8,128)(2,1)}) custom-call(s32[3]{0:T(128)} %pad_add_fusion.index, bf16[192,2304]{1,0:T(8,128)(2,1)} %bitcast.25, bf16[192,768]{1,0:T(8,128)(2,1)} %bitcast.37, bf16[288,768]{1,0:T(8,128)(2,1)} %bitcast.28), custom_call_target="tpu_custom_call" | custom-call | tf_op jit(solution)/shard_map/pack_rest/pallas_call | solution.py:656
  146.1 1.1 collective-permute-start.4
  147.3 0.8 collective-permute-start.7
  148.1 2.3 collective-permute-done.7.second_other
  150.5 1.2 copy-done.7
  151.6 7.5 %forward_attention.1 = (bf16[256,768]{1,0:T(8,128)(2,1)S(1)}, f32[2,768]{1,0:T(2,128)S(1)}, bf16[768,2304]{1,0:T(8,128)(2,1)S(1)}) custom-call(s32[3]{0:T(128)S(1)} %copy-done.20, bf16[2,128,768]{2,1,0:T(8,128)(2,1)S(1)} %bitcast.32, bf16[2,64,768]{2,1,0:T(8,128)(2,1)S(1)} %collective-permute-done.2.low, ...), custom_call_target="tpu_custom_call" | custom-call | flops 1400000000 | bytes 4666666 | tf_op jit(solution)/shard_map/forward_attention/pallas_call | solution.py:656
  159.1 1.7 copy-done
  160.8 8.0 %collective-permute-done.5.second = bf16[176,2304]{1,0:T(8,128)(2,1)S(1)} collective-permute-done((bf16[176,2304]{1,0:T(8,128)(2,1)}, bf16[176,2304]{1,0:T(8,128)(2,1)S(1)}, u32[]{:S(2)}, u32[]{:S(2)}) %collective-permute-start.5) | collective-permute-done | bytes 811040 | tf_op jit(solution)/shard_map/ppermute | solution.py:674
  168.8 6.3 %collective-permute-done.4.first = bf16[352,2304]{1,0:T(8,128)(2,1)S(1)} collective-permute-done((bf16[352,2304]{1,0:T(8,128)(2,1)}, bf16[352,2304]{1,0:T(8,128)(2,1)S(1)}, u32[]{:S(2)}, u32[]{:S(2)}) %collective-permute-start.4) | collective-permute-done | bytes 1622048 | tf_op jit(solution)/shard_map/ppermute | solution.py:674
  175.2 8.3 %collective-permute-start.8 = (bf16[352,2304]{1,0:T(8,128)(2,1)S(1)}, bf16[352,2304]{1,0:T(8,128)(2,1)S(1)}, u32[]{:S(2)}, u32[]{:S(2)}) collective-permute-start(bf16[352,2304]{1,0:T(8,128)(2,1)S(1)} %collective-permute-done.4.first), channel_id=1, source_target_pairs={{0,4},{1,5},{2,6},{3,7},{4,0},{5,1},{6,2},{7,3},{8,12},{9,13},{10,... | collective-permute-start | bytes 4866056 | tf_op jit(solution)/shard_map/ppermute | solution.py:674
  183.5 4.3 collective-permute-done.9.second_other
  187.7 6.7 %forward_mlp.1._ = bf16[2,128,768]{2,1,0:T(8,128)(2,1)S(1)} custom-call(s32[3]{0:T(128)S(1)} %copy-done.20, bf16[2,128,768]{2,1,0:T(8,128)(2,1)S(1)} %bitcast.33, bf16[256,768]{1,0:T(8,128)(2,1)S(1)} %get-tuple-element.113.o, f32[2,768]{1,0:T(2,128)S(1)} %get-tuple-element.114.gains, bf16[192,2304]{1,0:T(8,128)(2,1)S(1)} %bitcast.27, ...), custom_call_target="tpu_custom_call" | custom-call | flops 1800000000 | bytes 6000000 | tf_op jit(solution)/shard_map/forward_mlp/pallas_call | solution.py:656
  194.5 4.7 collective-permute-start.10
  199.2 8.1 %collective-permute-done.10.other_own = bf16[2,128,768]{2,1,0:T(8,128)(2,1)S(1)} collective-permute-done((bf16[2,128,768]{2,1,0:T(8,128)(2,1)S(1)}, bf16[2,128,768]{2,1,0:T(8,128)(2,1)S(1)}, u32[]{:S(2)}, u32[]{:S(2)}) %collective-permute-start.10) | collective-permute-done | bytes 393248 | tf_op jit(solution)/shard_map/ppermute | solution.py:830
  207.3 3.1 collective-permute-start.12
  210.4 6.6 %collective-permute-start.11 = (bf16[2,64,768]{2,1,0:T(8,128)(2,1)S(1)}, bf16[2,64,768]{2,1,0:T(8,128)(2,1)S(1)}, u32[]{:S(2)}, u32[]{:S(2)}) collective-permute-start(bf16[2,64,768]{2,1,0:T(8,128)(2,1)S(1)} %get-tuple-element.205), channel_id=1, source_target_pairs={{0,4},{4,8},{8,12},{12,16},{16,20},{20,24},{24,28},{28,32},{32,36}... | collective-permute-start | bytes 589832 | tf_op jit(solution)/shard_map/ppermute | solution.py:702
  217.0 198.7 %assemble_weights.1 = (bf16[768,2304]{1,0:T(8,128)(2,1)}, bf16[768,768]{1,0:T(8,128)(2,1)}, bf16[1152,768]{1,0:T(8,128)(2,1)}) custom-call(s32[3]{0:T(128)} %pad_add_fusion.index, bf16[192,2304]{1,0:T(8,128)(2,1)} %bitcast.26, bf16[192,768]{1,0:T(8,128)(2,1)} %bitcast.38, bf16[288,768]{1,0:T(8,128)(2,1)} %bitcast.29, bf16[352,2304]{1,0:T(8,128)(2,1)} %copy-done.3, ...), custom_call_target="tpu_custom_call" | custom-call | flops 1800000000 | bytes 6000000 | tf_op jit(solution)/shard_map/assemble_weights/pallas_call | solution.py:656
  415.8 23.9 %layer_turn.1 = (bf16[2,128,768]{2,1,0:T(8,128)(2,1)}, bf16[256,768]{1,0:T(8,128)(2,1)S(1)}, bf16[512,768]{1,0:T(8,128)(2,1)S(1)}, bf16[512,768]{1,0:T(8,128)(2,...) custom-call(s32[1]{0:T(128)} %bitcast.flag_ref, ...), custom_call_target="tpu_custom_call" | custom-call | flops 6000000000 | bytes 20000000 | tf_op jit(solution)/shard_map/layer_turn/pallas_call | solution.py:656
  439.8 2.4 collective-permute-start.13
  442.2 2.0 collective-permute-start.14
  444.2 2.7 collective-permute-done.13.from_low
  446.9 4.4 collective-permute-done.14.from_high
  451.3 1.4 copy-done.14
  452.7 2.2 layer_source.1
  454.9 1.5 collective-permute-start.15
  456.4 8.6 %collective-permute-done.15.incoming = bf16[2,128,768]{2,1,0:T(8,128)(2,1)S(1)} collective-permute-done((bf16[2,128,768]{2,1,0:T(8,128)(2,1)S(1)}, bf16[2,128,768]{2,1,0:T(8,128)(2,1)S(1)}, u32[]{:S(2)}, u32[]{:S(2)}) %collective-permute-start.15) | collective-permute-done | bytes 393248 | tf_op jit(solution)/shard_map/ppermute | solution.py:850
  465.1 11.8 %layer_back.1 = (bf16[256,768]{1,0:T(8,128)(2,1)S(1)}, bf16[256,2304]{1,0:T(8,128)(2,1)S(1)}, bf16[256,768]{1,0:T(8,128)(2,1)S(1)}, bf16[256,768]{1,0:T(8,128)(2...) custom-call(s32[1]{0:T(128)} %bitcast.flag_ref, ...), custom_call_target="tpu_custom_call" | custom-call | flops 3000000000 | bytes 10000000 | tf_op jit(solution)/shard_map/layer_back/pallas_call | solution.py:656
  476.9 5.6 collective-permute-start.16
  482.5 1.9 collective-permute-start.17
  484.5 7.0 %weight_grads.1 = (bf16[4,192,2304]{2,1,0:T(8,128)(2,1)S(1)}, bf16[4,192,2304]{2,1,0:T(8,128)(2,1)S(1)}) custom-call(s32[3]{0:T(128)S(1)} %copy-done.21, bf16[256,1152]{1,0:T(8,128)(2,1)S(1)} %get-tuple-element.140.m_ref, bf16[256,768]{1,0:T(8,128)(2,1)S(1)} %get-tuple-element.141.grad_ref, bf16[256,768]{1,0:T(8,128)(2,1)S(1)} %get-tuple-element.142.b_ref, ...), custom_call_target="tpu_custom_call" | custom-call | flops 1600000000 | bytes 5333333 | tf_op jit(solution)/shard_map/weight_grads/pallas_call | solution.py:656
  491.6 5.0 layer_source_grads.1
  496.6 0.8 collective-permute-start.19
  497.8 1.3 rest_core_sum.1
  499.2 1.7 collective-permute-done.19.other
  500.9 1.0 qkv_core_sum.1
  502.0 1.7 collective-permute-start.21
  503.7 6.3 %collective-permute-start.22 = (bf16[4,48,2304]{2,1,0:T(8,128)(2,1)S(1)}, bf16[4,48,2304]{2,1,0:T(8,128)(2,1)S(1)}, u32[]{:S(2)}, u32[]{:S(2)}) collective-permute-start(bf16[4,48,2304]{2,1,0:T(8,128)(2,1)S(1)} %get-tuple-element.161), channel_id=1, source_target_pairs={{0,16},{1,17},{2,18},{3,19},{4,20},{5,21},{6,22},{7,23},{8,24},{9,... | collective-permute-start | bytes 2654216 | tf_op jit(solution)/shard_map/ppermute | solution.py:674
  510.6 14.5 %collective-permute-done.20.b = bf16[96,2432]{1,0:T(8,128)(2,1)S(1)} collective-permute-done((bf16[96,2432]{1,0:T(8,128)(2,1)S(1)}, bf16[96,2432]{1,0:T(8,128)(2,1)S(1)}, u32[]{:S(2)}, u32[]{:S(2)}) %collective-permute-start.20) | collective-permute-done | bytes 466976 | tf_op jit(solution)/shard_map/ppermute | solution.py:674
  525.2 3.4 collective-permute-done.21.a
  528.6 19.8 %collective-permute-done.22.b = bf16[4,48,2304]{2,1,0:T(8,128)(2,1)S(1)} collective-permute-done((bf16[4,48,2304]{2,1,0:T(8,128)(2,1)S(1)}, bf16[4,48,2304]{2,1,0:T(8,128)(2,1)S(1)}, u32[]{:S(2)}, u32[]{:S(2)}) %collective-permute-start.22) | collective-permute-done | bytes 884768 | tf_op jit(solution)/shard_map/ppermute | solution.py:674
  548.4 1.0 rest_z_sum.1
  549.4 0.9 qkv_y_sum.1
  550.6 3.7 collective-permute-start.25
  554.2 3.6 collective-permute-start.30
  557.8 2.3 collective-permute-done.30.q2
  560.1 2.5 collective-permute-done.31.q3
  563.6 2.3 collective-permute-start.32
  565.9 6.7 %collective-permute-done.32.b = bf16[48,3584]{1,0:T(8,128)(2,1)S(1)} collective-permute-done((bf16[48,3584]{1,0:T(8,128)(2,1)S(1)}, bf16[48,3584]{1,0:T(8,128)(2,1)S(1)}, u32[]{:S(2)}, u32[]{:S(2)}) %collective-permute-start.32) | collective-permute-done | bytes 344096 | tf_op jit(solution)/shard_map/ppermute | solution.py:674
  572.7 0.8 collective-permute-start.35
  573.5 2.2 collective-permute-start.34
  575.7 0.8 collective-permute-start.33
  576.4 3.4 collective-permute-start.36
  580.0 6.1 %collective-permute-start.39 = (bf16[48,3584]{1,0:T(8,128)(2,1)S(1)}, bf16[48,3584]{1,0:T(8,128)(2,1)S(1)}, u32[]{:S(2)}, u32[]{:S(2)}) collective-permute-start(bf16[48,3584]{1,0:T(8,128)(2,1)S(1)} %collective-permute-done.35.refs_3_), channel_id=1, source_target_pairs={{0,4},{1,5},{2,6},{3,7},{4,0},{5,1},{6,2},{7,3},{8,12},{9,13},{10,... | collective-permute-start | bytes 1032200 | tf_op jit(solution)/shard_map/ppermute | solution.py:674
  586.1 3.2 collective-permute-start.38
  589.2 2.3 collective-permute-done.33.refs_1_
  591.6 1.3 collective-permute-start.37
  592.9 1.3 collective-permute-done.37.refs_5_
  594.1 3.0 final_shard.1
  (101 shorter events, 7.0 us)
Async XLA Ops:
  0.6 68.8 %copy-start.23 = (s32[2,1,4]{2,1,0:T(1,128)S(1)}, s32[2,1,4]{2,1,0:T(1,128)}, u32[]{:S(2)}) copy-start(s32[2,1,4]{2,1,0:T(1,128)} %param.11) | copy-start | bytes 100
  56.9 89.2 %collective-permute-start = (bf16[192,2432]{1,0:T(8,128)(2,1)}, bf16[192,2432]{1,0:T(8,128)(2,1)S(1)}, u32[]{:S(2)}, u32[]{:S(2)}) collective-permute-start(bf16[192,2432]{1,0:T(8,128)(2,1)} %get-tuple-element.94), channel_id=1, source_target_pairs={{0,1},{1,2},{2,3},{3,0},{4,7},{5,4},{6,5},{7,6},{8,9},{9,10},{10,1... | collective-permute-start | bytes 2801672 | tf_op jit(solution)/shard_map/ppermute | solution.py:674
  61.0 89.4 %copy-start.6 = (bf16[2,1,128,768]{3,2,1,0:T(8,128)(2,1)S(1)}, bf16[2,1,128,768]{3,2,1,0:T(8,128)(2,1)}, u32[]{:S(2)}) copy-start(bf16[2,1,128,768]{3,2,1,0:T(8,128)(2,1)} %param.9) | copy-start | bytes 1179652
  61.1 89.4 %copy-start.20 = (s32[3]{0:T(128)S(1)}, s32[3]{0:T(128)}, u32[]{:S(2)}) copy-start(s32[3]{0:T(128)} %pad_add_fusion.index) | copy-start | bytes 40
  61.1 89.4 %copy-start.22 = (bf16[16,128]{1,0:T(8,128)(2,1)S(1)}, bf16[16,128]{1,0:T(8,128)(2,1)}, u32[]{:S(2)}) copy-start(bf16[16,128]{1,0:T(8,128)(2,1)} %pad.9.gains.gain_tile) | copy-start | bytes 12292
  61.9 84.2 %collective-permute-start.2 = (bf16[2,64,768]{2,1,0:T(8,128)(2,1)}, bf16[2,64,768]{2,1,0:T(8,128)(2,1)S(1)}, u32[]{:S(2)}, u32[]{:S(2)}) collective-permute-start(bf16[2,64,768]{2,1,0:T(8,128)(2,1)} %get-tuple-element.101), channel_id=1, source_target_pairs={{0,4},{4,8},{8,12},{12,16},{16,20},{20,24},{24,28},{28,32},{32,36}... | collective-permute-start | bytes 589832 | tf_op jit(solution)/shard_map/ppermute | solution.py:711
  64.8 81.2 %collective-permute-start.3 = (bf16[2,64,768]{2,1,0:T(8,128)(2,1)}, bf16[2,64,768]{2,1,0:T(8,128)(2,1)S(1)}, u32[]{:S(2)}, u32[]{:S(2)}) collective-permute-start(bf16[2,64,768]{2,1,0:T(8,128)(2,1)} %get-tuple-element.102), channel_id=1, source_target_pairs={{4,0},{8,4},{12,8},{16,12},{20,16},{24,20},{28,24},{32,28},{36,32}... | collective-permute-start | bytes 589832 | tf_op jit(solution)/shard_map/ppermute | solution.py:711
  66.8 79.3 %collective-permute-start.1 = (bf16[96,2432]{1,0:T(8,128)(2,1)}, bf16[96,2432]{1,0:T(8,128)(2,1)S(1)}, u32[]{:S(2)}, u32[]{:S(2)}) collective-permute-start(bf16[96,2432]{1,0:T(8,128)(2,1)} %get-tuple-element.95), channel_id=1, source_target_pairs={{0,2},{1,3},{2,0},{3,1},{4,6},{5,7},{6,4},{7,5},{8,10},{9,11},{10,... | collective-permute-start | bytes 1400840 | tf_op jit(solution)/shard_map/ppermute | solution.py:674
  69.6 80.8 %copy-start.17 = (f32[256,128]{1,0:T(8,128)S(1)}, f32[256,128]{1,0:T(8,128)}, u32[]{:S(2)}) copy-start(f32[256,128]{1,0:T(8,128)} %pad_maximum_fusion.1.cos_ref) | copy-start | bytes 393220
  146.0 13.1 %copy-start.11 = (f32[2,256,256]{2,1,0:T(8,128)}, f32[2,256,256]{2,1,0:T(8,128)S(1)}, u32[]{:S(2)}) copy-start(f32[2,256,256]{2,1,0:T(8,128)S(1)} %pad_maximum_fusion.bias_ref) | copy-start | bytes 1572868
  146.1 41.6 %copy-start.2 = (bf16[1,192,2304]{2,1,0:T(8,128)(2,1)S(1)}, bf16[1,192,2304]{2,1,0:T(8,128)(2,1)}, u32[]{:S(2)}) copy-start(bf16[1,192,2304]{2,1,0:T(8,128)(2,1)} %param.16) | copy-start | bytes 2654212
  146.1 41.6 %copy-start.5 = (bf16[1,288,768]{2,1,0:T(8,128)(2,1)S(1)}, bf16[1,288,768]{2,1,0:T(8,128)(2,1)}, u32[]{:S(2)}) copy-start(bf16[1,288,768]{2,1,0:T(8,128)(2,1)} %param.17) | copy-start | bytes 1327108
  146.1 29.1 %collective-permute-start.4 = (bf16[352,2304]{1,0:T(8,128)(2,1)}, bf16[352,2304]{1,0:T(8,128)(2,1)S(1)}, u32[]{:S(2)}, u32[]{:S(2)}) collective-permute-start(bf16[352,2304]{1,0:T(8,128)(2,1)} %get-tuple-element.105), channel_id=1, source_target_pairs={{0,1},{1,2},{2,3},{3,0},{4,7},{5,4},{6,5},{7,6},{8,9},{9,10},{10,1... | collective-permute-start | bytes 4866056 | tf_op jit(solution)/shard_map/ppermute | solution.py:674
  147.2 3.2 collective-permute-start.6
  147.2 21.6 %collective-permute-start.5 = (bf16[176,2304]{1,0:T(8,128)(2,1)}, bf16[176,2304]{1,0:T(8,128)(2,1)S(1)}, u32[]{:S(2)}, u32[]{:S(2)}) collective-permute-start(bf16[176,2304]{1,0:T(8,128)(2,1)} %get-tuple-element.106), channel_id=1, source_target_pairs={{0,2},{1,3},{2,0},{3,1},{4,6},{5,7},{6,4},{7,5},{8,10},{9,11},{10,... | collective-permute-start | bytes 2433032 | tf_op jit(solution)/shard_map/ppermute | solution.py:674
  147.3 3.1 collective-permute-start.7
  150.4 1.2 copy-start.7
  151.6 36.1 %copy-start.10 = (bf16[1,192,768]{2,1,0:T(8,128)(2,1)S(1)}, bf16[1,192,768]{2,1,0:T(8,128)(2,1)}, u32[]{:S(2)}) copy-start(bf16[1,192,768]{2,1,0:T(8,128)(2,1)} %param.14) | copy-start | bytes 884740
  159.1 1.8 copy-start
  168.8 25.6 %copy-start.8 = (bf16[176,2304]{1,0:T(8,128)(2,1)}, bf16[176,2304]{1,0:T(8,128)(2,1)S(1)}, u32[]{:S(2)}) copy-start(bf16[176,2304]{1,0:T(8,128)(2,1)S(1)} %collective-permute-done.5.second) | copy-start | bytes 2433028
  175.2 19.3 %copy-start.3 = (bf16[352,2304]{1,0:T(8,128)(2,1)}, bf16[352,2304]{1,0:T(8,128)(2,1)S(1)}, u32[]{:S(2)}) copy-start(bf16[352,2304]{1,0:T(8,128)(2,1)S(1)} %collective-permute-done.4.first) | copy-start | bytes 4866052
  175.2 12.6 %collective-permute-start.8 = (bf16[352,2304]{1,0:T(8,128)(2,1)S(1)}, bf16[352,2304]{1,0:T(8,128)(2,1)S(1)}, u32[]{:S(2)}, u32[]{:S(2)}) collective-permute-start(bf16[352,2304]{1,0:T(8,128)(2,1)S(1)} %collective-permute-done.4.first), channel_id=1, source_target_pairs={{0,4},{1,5},{2,6},{3,7},{4,0},{5,1},{6,2},{7,3},{8,12},{9,13},{10,... | collective-permute-start | bytes 4866056 | tf_op jit(solution)/shard_map/ppermute | solution.py:674
  183.4 4.3 collective-permute-start.9
  187.7 6.8 %copy-start.9 = (bf16[176,2304]{1,0:T(8,128)(2,1)}, bf16[176,2304]{1,0:T(8,128)(2,1)S(1)}, u32[]{:S(2)}) copy-start(bf16[176,2304]{1,0:T(8,128)(2,1)S(1)} %collective-permute-done.9.second_other) | copy-start | bytes 2433028
  187.7 6.8 %copy-start.4 = (bf16[352,2304]{1,0:T(8,128)(2,1)}, bf16[352,2304]{1,0:T(8,128)(2,1)S(1)}, u32[]{:S(2)}) copy-start(bf16[352,2304]{1,0:T(8,128)(2,1)S(1)} %collective-permute-done.8.first_other) | copy-start | bytes 4866052
  194.5 4.7 copy-start.13
  194.5 12.8 %collective-permute-start.10 = (bf16[2,128,768]{2,1,0:T(8,128)(2,1)S(1)}, bf16[2,128,768]{2,1,0:T(8,128)(2,1)S(1)}, u32[]{:S(2)}, u32[]{:S(2)}) collective-permute-start(bf16[2,128,768]{2,1,0:T(8,128)(2,1)S(1)} %forward_mlp.1._), channel_id=1, source_target_pairs={{0,64},{1,65},{2,66},{3,67},{4,68},{5,69},{6,70},{7,71},{8,72},{9,... | collective-permute-start | bytes 1179656 | tf_op jit(solution)/shard_map/ppermute | solution.py:830
  207.3 208.5 %collective-permute-start.12 = (bf16[2,64,768]{2,1,0:T(8,128)(2,1)S(1)}, bf16[2,64,768]{2,1,0:T(8,128)(2,1)S(1)}, u32[]{:S(2)}, u32[]{:S(2)}) collective-permute-start(bf16[2,64,768]{2,1,0:T(8,128)(2,1)S(1)} %get-tuple-element.204), channel_id=1, source_target_pairs={{4,0},{8,4},{12,8},{16,12},{20,16},{24,20},{28,24},{32,28},{36,32}... | collective-permute-start | bytes 589832 | tf_op jit(solution)/shard_map/ppermute | solution.py:703
  210.4 205.4 %collective-permute-start.11 = (bf16[2,64,768]{2,1,0:T(8,128)(2,1)S(1)}, bf16[2,64,768]{2,1,0:T(8,128)(2,1)S(1)}, u32[]{:S(2)}, u32[]{:S(2)}) collective-permute-start(bf16[2,64,768]{2,1,0:T(8,128)(2,1)S(1)} %get-tuple-element.205), channel_id=1, source_target_pairs={{0,4},{4,8},{8,12},{12,16},{16,20},{20,24},{24,28},{28,32},{32,36}... | collective-permute-start | bytes 589832 | tf_op jit(solution)/shard_map/ppermute | solution.py:702
  217.0 198.8 %copy-start.12 = (f32[2,256,256]{2,1,0:T(8,128)S(1)}, f32[2,256,256]{2,1,0:T(8,128)}, u32[]{:S(2)}) copy-start(f32[2,256,256]{2,1,0:T(8,128)} %copy-done.11) | copy-start | bytes 1572868
  217.0 198.8 %copy-start.18 = (f32[256,128]{1,0:T(8,128)S(1)}, f32[256,128]{1,0:T(8,128)}, u32[]{:S(2)}) copy-start(f32[256,128]{1,0:T(8,128)} %pad_maximum_fusion.1.cos_ref) | copy-start | bytes 393220
  217.0 198.8 %copy-start.19 = (bf16[2,1,128,768]{3,2,1,0:T(8,128)(2,1)S(1)}, bf16[2,1,128,768]{3,2,1,0:T(8,128)(2,1)}, u32[]{:S(2)}) copy-start(bf16[2,1,128,768]{3,2,1,0:T(8,128)(2,1)} %param.10) | copy-start | bytes 1179652
  415.8 35.5 %copy-start.1 = (bf16[768,2304]{1,0:T(8,128)(2,1)S(1)}, bf16[768,2304]{1,0:T(8,128)(2,1)}, u32[]{:S(2)}) copy-start(bf16[768,2304]{1,0:T(8,128)(2,1)} %copy-done) | copy-start | bytes 10616836
  439.8 7.1 %collective-permute-start.13 = (bf16[2,64,1536]{2,1,0:T(8,128)(2,1)S(1)}, bf16[2,64,1536]{2,1,0:T(8,128)(2,1)S(1)}, u32[]{:S(2)}, u32[]{:S(2)}) collective-permute-start(bf16[2,64,1536]{2,1,0:T(8,128)(2,1)S(1)} %get-tuple-element.126), channel_id=1, source_target_pairs={{0,4},{4,8},{8,12},{12,16},{16,20},{20,24},{24,28},{28,32},{32,36}... | collective-permute-start | bytes 1179656 | tf_op jit(solution)/shard_map/ppermute | solution.py:711
  442.2 9.1 %collective-permute-start.14 = (bf16[2,64,1536]{2,1,0:T(8,128)(2,1)S(1)}, bf16[2,64,1536]{2,1,0:T(8,128)(2,1)S(1)}, u32[]{:S(2)}, u32[]{:S(2)}) collective-permute-start(bf16[2,64,1536]{2,1,0:T(8,128)(2,1)S(1)} %get-tuple-element.127), channel_id=1, source_target_pairs={{4,0},{8,4},{12,8},{16,12},{20,16},{24,20},{28,24},{32,28},{36,32}... | collective-permute-start | bytes 1179656 | tf_op jit(solution)/shard_map/ppermute | solution.py:711
  451.3 1.4 copy-start.14
  452.7 12.4 %copy-start.15 = (bf16[768,768]{1,0:T(8,128)(2,1)S(1)}, bf16[768,768]{1,0:T(8,128)(2,1)}, u32[]{:S(2)}) copy-start(bf16[768,768]{1,0:T(8,128)(2,1)} %get-tuple-element.118.proj_hbm) | copy-start | bytes 3538948
  452.7 12.4 %copy-start.16 = (f32[256,1152]{1,0:T(8,128)S(1)}, f32[256,1152]{1,0:T(8,128)}, u32[]{:S(2)}) copy-start(f32[256,1152]{1,0:T(8,128)} %get-tuple-element.134.right_hbm) | copy-start | bytes 3538948
  454.9 10.2 %collective-permute-start.15 = (bf16[2,128,768]{2,1,0:T(8,128)(2,1)S(1)}, bf16[2,128,768]{2,1,0:T(8,128)(2,1)S(1)}, u32[]{:S(2)}, u32[]{:S(2)}) collective-permute-start(bf16[2,128,768]{2,1,0:T(8,128)(2,1)S(1)} %layer_source.1), channel_id=1, source_target_pairs={{64,0},{65,1},{66,2},{67,3},{68,4},{69,5},{70,6},{71,7},{72,8},{73... | collective-permute-start | bytes 1179656 | tf_op jit(solution)/shard_map/ppermute | solution.py:850
  465.1 19.4 %copy-start.21 = (s32[3]{0:T(128)S(1)}, s32[3]{0:T(128)}, u32[]{:S(2)}) copy-start(s32[3]{0:T(128)} %pad_add_fusion.index) | copy-start | bytes 40
  476.9 14.5 %collective-permute-start.16 = (bf16[2,64,1536]{2,1,0:T(8,128)(2,1)S(1)}, bf16[2,64,1536]{2,1,0:T(8,128)(2,1)S(1)}, u32[]{:S(2)}, u32[]{:S(2)}) collective-permute-start(bf16[2,64,1536]{2,1,0:T(8,128)(2,1)S(1)} %get-tuple-element.138), channel_id=1, source_target_pairs={{0,4},{4,8},{8,12},{12,16},{16,20},{20,24},{24,28},{28,32},{32,36}... | collective-permute-start | bytes 1179656 | tf_op jit(solution)/shard_map/ppermute | solution.py:711
  482.5 9.1 %collective-permute-start.17 = (bf16[2,64,1536]{2,1,0:T(8,128)(2,1)S(1)}, bf16[2,64,1536]{2,1,0:T(8,128)(2,1)S(1)}, u32[]{:S(2)}, u32[]{:S(2)}) collective-permute-start(bf16[2,64,1536]{2,1,0:T(8,128)(2,1)S(1)} %get-tuple-element.139), channel_id=1, source_target_pairs={{4,0},{8,4},{12,8},{16,12},{20,16},{24,20},{28,24},{32,28},{36,32}... | collective-permute-start | bytes 1179656 | tf_op jit(solution)/shard_map/ppermute | solution.py:711
  491.6 6.2 %collective-permute-start.18 = (bf16[4,192,2304]{2,1,0:T(8,128)(2,1)S(1)}, bf16[4,192,2304]{2,1,0:T(8,128)(2,1)S(1)}, u32[]{:S(2)}, u32[]{:S(2)}) collective-permute-start(bf16[4,192,2304]{2,1,0:T(8,128)(2,1)S(1)} %get-tuple-element.152), channel_id=1, source_target_pairs={{0,4},{1,5},{2,6},{3,7},{4,0},{5,1},{6,2},{7,3},{8,12},{9,13},{10,... | collective-permute-start | bytes 10616840 | tf_op jit(solution)/shard_map/ppermute | solution.py:674
  496.6 4.3 collective-permute-start.19
  501.9 23.2 %collective-permute-start.20 = (bf16[96,2432]{1,0:T(8,128)(2,1)S(1)}, bf16[96,2432]{1,0:T(8,128)(2,1)S(1)}, u32[]{:S(2)}, u32[]{:S(2)}) collective-permute-start(bf16[96,2432]{1,0:T(8,128)(2,1)S(1)} %get-tuple-element.158), channel_id=1, source_target_pairs={{0,1},{1,2},{2,3},{3,0},{4,5},{5,6},{6,7},{7,4},{8,9},{9,10},{10,1... | collective-permute-start | bytes 1400840 | tf_op jit(solution)/shard_map/ppermute | solution.py:674
  502.0 26.6 %collective-permute-start.21 = (bf16[4,48,2304]{2,1,0:T(8,128)(2,1)S(1)}, bf16[4,48,2304]{2,1,0:T(8,128)(2,1)S(1)}, u32[]{:S(2)}, u32[]{:S(2)}) collective-permute-start(bf16[4,48,2304]{2,1,0:T(8,128)(2,1)S(1)} %get-tuple-element.160), channel_id=1, source_target_pairs={{0,8},{1,9},{2,10},{3,11},{4,12},{5,13},{6,14},{7,15},{8,16},{9,17... | collective-permute-start | bytes 2654216 | tf_op jit(solution)/shard_map/ppermute | solution.py:674
  503.7 44.7 %collective-permute-start.22 = (bf16[4,48,2304]{2,1,0:T(8,128)(2,1)S(1)}, bf16[4,48,2304]{2,1,0:T(8,128)(2,1)S(1)}, u32[]{:S(2)}, u32[]{:S(2)}) collective-permute-start(bf16[4,48,2304]{2,1,0:T(8,128)(2,1)S(1)} %get-tuple-element.161), channel_id=1, source_target_pairs={{0,16},{1,17},{2,18},{3,19},{4,20},{5,21},{6,22},{7,23},{8,24},{9,... | collective-permute-start | bytes 2654216 | tf_op jit(solution)/shard_map/ppermute | solution.py:674
  510.0 38.4 %collective-permute-start.23 = (bf16[4,48,2304]{2,1,0:T(8,128)(2,1)S(1)}, bf16[4,48,2304]{2,1,0:T(8,128)(2,1)S(1)}, u32[]{:S(2)}, u32[]{:S(2)}) collective-permute-start(bf16[4,48,2304]{2,1,0:T(8,128)(2,1)S(1)} %get-tuple-element.162), channel_id=1, source_target_pairs={{0,24},{1,25},{2,26},{3,27},{4,28},{5,29},{6,30},{7,31},{8,0},{9,1... | collective-permute-start | bytes 2654216 | tf_op jit(solution)/shard_map/ppermute | solution.py:674
  510.1 39.3 %collective-permute-start.27 = (bf16[96,2432]{1,0:T(8,128)(2,1)S(1)}, bf16[96,2432]{1,0:T(8,128)(2,1)S(1)}, u32[]{:S(2)}, u32[]{:S(2)}) collective-permute-start(bf16[96,2432]{1,0:T(8,128)(2,1)S(1)} %get-tuple-element.169), channel_id=1, source_target_pairs={{0,2},{1,3},{2,0},{3,1},{4,6},{5,7},{6,4},{7,5},{8,10},{9,11},{10,... | collective-permute-start | bytes 1400840 | tf_op jit(solution)/shard_map/ppermute | solution.py:674
  525.1 24.3 %collective-permute-start.28 = (bf16[96,2432]{1,0:T(8,128)(2,1)S(1)}, bf16[96,2432]{1,0:T(8,128)(2,1)S(1)}, u32[]{:S(2)}, u32[]{:S(2)}) collective-permute-start(bf16[96,2432]{1,0:T(8,128)(2,1)S(1)} %get-tuple-element.170), channel_id=1, source_target_pairs={{0,3},{1,0},{2,1},{3,2},{4,7},{5,4},{6,5},{7,6},{8,11},{9,8},{10,9... | collective-permute-start | bytes 1400840 | tf_op jit(solution)/shard_map/ppermute | solution.py:674
  550.3 7.5 %collective-permute-start.29 = (bf16[48,1280]{1,0:T(8,128)(2,1)S(1)}, bf16[48,1280]{1,0:T(8,128)(2,1)S(1)}, u32[]{:S(2)}, u32[]{:S(2)}) collective-permute-start(bf16[48,1280]{1,0:T(8,128)(2,1)S(1)} %get-tuple-element.172), channel_id=1, source_target_pairs={{0,8},{1,9},{2,10},{3,11},{4,12},{5,13},{6,14},{7,15},{8,16},{9,17... | collective-permute-start | bytes 368648 | tf_op jit(solution)/shard_map/ppermute | solution.py:674
  550.6 12.1 %collective-permute-start.24 = (bf16[48,2304]{1,0:T(8,128)(2,1)S(1)}, bf16[48,2304]{1,0:T(8,128)(2,1)S(1)}, u32[]{:S(2)}, u32[]{:S(2)}) collective-permute-start(bf16[48,2304]{1,0:T(8,128)(2,1)S(1)} %get-tuple-element.164), channel_id=1, source_target_pairs={{0,1},{1,2},{2,3},{3,0},{4,5},{5,6},{6,7},{7,4},{8,9},{9,10},{10,1... | collective-permute-start | bytes 663560 | tf_op jit(solution)/shard_map/ppermute | solution.py:674
  550.6 12.7 %collective-permute-start.25 = (bf16[48,2304]{1,0:T(8,128)(2,1)S(1)}, bf16[48,2304]{1,0:T(8,128)(2,1)S(1)}, u32[]{:S(2)}, u32[]{:S(2)}) collective-permute-start(bf16[48,2304]{1,0:T(8,128)(2,1)S(1)} %get-tuple-element.165), channel_id=1, source_target_pairs={{0,2},{1,3},{2,0},{3,1},{4,6},{5,7},{6,4},{7,5},{8,10},{9,11},{10,... | collective-permute-start | bytes 663560 | tf_op jit(solution)/shard_map/ppermute | solution.py:674
  554.2 9.2 %collective-permute-start.26 = (bf16[48,2304]{1,0:T(8,128)(2,1)S(1)}, bf16[48,2304]{1,0:T(8,128)(2,1)S(1)}, u32[]{:S(2)}, u32[]{:S(2)}) collective-permute-start(bf16[48,2304]{1,0:T(8,128)(2,1)S(1)} %get-tuple-element.166), channel_id=1, source_target_pairs={{0,3},{1,0},{2,1},{3,2},{4,7},{5,4},{6,5},{7,6},{8,11},{9,8},{10,9... | collective-permute-start | bytes 663560 | tf_op jit(solution)/shard_map/ppermute | solution.py:674
  554.2 5.8 collective-permute-start.30
  557.8 4.8 collective-permute-start.31
  563.6 9.0 %collective-permute-start.32 = (bf16[48,3584]{1,0:T(8,128)(2,1)S(1)}, bf16[48,3584]{1,0:T(8,128)(2,1)S(1)}, u32[]{:S(2)}, u32[]{:S(2)}) collective-permute-start(bf16[48,3584]{1,0:T(8,128)(2,1)S(1)} %joint_sum.1.a), channel_id=1, source_target_pairs={{0,32},{1,33},{2,34},{3,35},{4,36},{5,37},{6,38},{7,39},{8,40},{9,... | collective-permute-start | bytes 1032200 | tf_op jit(solution)/shard_map/ppermute | solution.py:674
  572.7 7.3 %collective-permute-start.35 = (bf16[48,3584]{1,0:T(8,128)(2,1)S(1)}, bf16[48,3584]{1,0:T(8,128)(2,1)S(1)}, u32[]{:S(2)}, u32[]{:S(2)}) collective-permute-start(bf16[48,3584]{1,0:T(8,128)(2,1)S(1)} %pair_sum.1.refs_0_), channel_id=1, source_target_pairs={{0,24},{1,25},{2,26},{3,27},{4,28},{5,29},{6,30},{7,31},{8,0},{9,1... | collective-permute-start | bytes 1032200 | tf_op jit(solution)/shard_map/ppermute | solution.py:674
  573.5 12.6 %collective-permute-start.34 = (bf16[48,3584]{1,0:T(8,128)(2,1)S(1)}, bf16[48,3584]{1,0:T(8,128)(2,1)S(1)}, u32[]{:S(2)}, u32[]{:S(2)}) collective-permute-start(bf16[48,3584]{1,0:T(8,128)(2,1)S(1)} %pair_sum.1.refs_0_), channel_id=1, source_target_pairs={{0,16},{1,17},{2,18},{3,19},{4,20},{5,21},{6,22},{7,23},{8,24},{9,... | collective-permute-start | bytes 1032200 | tf_op jit(solution)/shard_map/ppermute | solution.py:674
  575.7 15.9 %collective-permute-start.33 = (bf16[48,3584]{1,0:T(8,128)(2,1)S(1)}, bf16[48,3584]{1,0:T(8,128)(2,1)S(1)}, u32[]{:S(2)}, u32[]{:S(2)}) collective-permute-start(bf16[48,3584]{1,0:T(8,128)(2,1)S(1)} %pair_sum.1.refs_0_), channel_id=1, source_target_pairs={{0,8},{1,9},{2,10},{3,11},{4,12},{5,13},{6,14},{7,15},{8,16},{9,17... | collective-permute-start | bytes 1032200 | tf_op jit(solution)/shard_map/ppermute | solution.py:674
  576.4 16.4 %collective-permute-start.36 = (bf16[48,3584]{1,0:T(8,128)(2,1)S(1)}, bf16[48,3584]{1,0:T(8,128)(2,1)S(1)}, u32[]{:S(2)}, u32[]{:S(2)}) collective-permute-start(bf16[48,3584]{1,0:T(8,128)(2,1)S(1)} %pair_sum.1.refs_0_), channel_id=1, source_target_pairs={{0,4},{1,5},{2,6},{3,7},{4,0},{5,1},{6,2},{7,3},{8,12},{9,13},{10,... | collective-permute-start | bytes 1032200 | tf_op jit(solution)/shard_map/ppermute | solution.py:674
  580.0 12.9 %collective-permute-start.39 = (bf16[48,3584]{1,0:T(8,128)(2,1)S(1)}, bf16[48,3584]{1,0:T(8,128)(2,1)S(1)}, u32[]{:S(2)}, u32[]{:S(2)}) collective-permute-start(bf16[48,3584]{1,0:T(8,128)(2,1)S(1)} %collective-permute-done.35.refs_3_), channel_id=1, source_target_pairs={{0,4},{1,5},{2,6},{3,7},{4,0},{5,1},{6,2},{7,3},{8,12},{9,13},{10,... | collective-permute-start | bytes 1032200 | tf_op jit(solution)/shard_map/ppermute | solution.py:674
  586.1 6.8 %collective-permute-start.38 = (bf16[48,3584]{1,0:T(8,128)(2,1)S(1)}, bf16[48,3584]{1,0:T(8,128)(2,1)S(1)}, u32[]{:S(2)}, u32[]{:S(2)}) collective-permute-start(bf16[48,3584]{1,0:T(8,128)(2,1)S(1)} %collective-permute-done.34.refs_2_), channel_id=1, source_target_pairs={{0,4},{1,5},{2,6},{3,7},{4,0},{5,1},{6,2},{7,3},{8,12},{9,13},{10,... | collective-permute-start | bytes 1032200 | tf_op jit(solution)/shard_map/ppermute | solution.py:674
  591.6 2.6 collective-permute-start.37
